TPU v7x, 256 devices: a whole 4x4x8 slice. The times are simulated.
256 devices in a mesh: row: 8 (over y_hi, x), col: 16 (over y_lo, z), pts: 2 (over core).
Axes of the slice: x: 4, y: 4 (y_hi: 2, y_lo: 2; y = y_hi * 2 + y_lo), z: 8, core: 2. Of those that a mesh axis runs over, the one named last changes fastest.
Arguments:
- green_panel: bfloat16 [4, 2, 512, 6144], P(None, None, 'col', 'pts'), may hold values from -6 to 6
- log_psd: float32 [2, 4, 3072], P('pts', None, ('row', 'col')), may hold values from -1.1 to 1.1
- observed: float32 [4, 2, 512, 512], P(None, None, 'row', 'col'), may hold values from -1 to 1
- pair_weights: int32 [512, 512], P('row', 'col'), may hold values from 0 to 4, as said below
Outputs:
- updated_log_psd: float32 [2, 4, 3072], P('pts', None, ('row', 'col'))
Inputs may be any that keep to these rules, and one draw needn't show every extreme that they name: pair_weights is 0 for pairs that are not listed and for every station paired with itself; the share of listed pairs differs from one block of 64 x 32 pairs (one index of row by one of col) to another, and some such blocks list no pair.
All inputs are finite; a program needn't handle non-finite values.
Results may differ from a plain program's by a relative error of at most 0.0014.
Values may be sent and summed in bfloat16 or wider, within the bound.
A program may use at most 64 MiB of HBM per device.

v0:
```python
import jax
import jax.numpy as jnp
from jax import lax
from jax.sharding import PartitionSpec as P

ITERS = 2


epsilon = 1e-06
descent = 0.1


def from_root(block, axis, source):
    block = jnp.where(lax.axis_index(axis) == source, block, jnp.zeros_like(block))
    return lax.psum(block, axis)


def pair_total(partial_value):
    return lax.psum(partial_value.astype(jnp.bfloat16), "pts").astype(jnp.float32)


def descend(log_field, gradient, entry_count):
    squares = lax.psum(jnp.sum(gradient * gradient), ("row", "col", "pts"))
    return log_field - descent * gradient / jnp.sqrt(squares / entry_count + epsilon)


def correlate(left_rows, weighted):
    half_a = left_rows.shape[1] // 2
    half_b = weighted.shape[1] // 2
    products = jnp.einsum("fan,fbn->fab", left_rows, weighted, preferred_element_type=jnp.float32)
    corr_real = products[:, :half_a, :half_b] + products[:, half_a:, half_b:]
    corr_imag = products[:, half_a:, :half_b] - products[:, :half_a, half_b:]
    return jnp.stack([corr_real, corr_imag], axis=1)


def adjoint_block(adjoint):
    adj_real = adjoint[:, 0]
    adj_imag = adjoint[:, 1]
    top_half = jnp.concatenate([adj_real, -adj_imag], axis=2)
    low_half = jnp.concatenate([adj_imag, adj_real], axis=2)
    return jnp.concatenate([top_half, low_half], axis=1)


def point_terms(adjoint, right_rows, left_rows, psd_field, quad_weight):
    accumulated = jnp.einsum(
        "fab,fbn->fan", adjoint_block(adjoint), right_rows, preferred_element_type=jnp.float32
    )
    return quad_weight * psd_field * jnp.sum(left_rows * accumulated, axis=1)


def body(green_panel, log_psd, observed, pair_weights):
    freq_count, comp_count, span_j, local_pts = green_panel.shape
    span_i = observed.shape[2]
    row_count = lax.axis_size("row")
    col_count = lax.axis_size("col")
    pts_count = lax.axis_size("pts")
    quad_weight = 1.0 / (pts_count * local_pts)
    entry_count = freq_count * pts_count * local_pts
    pair_scale = pair_weights.astype(jnp.float32)
    log_start = log_psd[0]
    group_ratio = col_count // row_count
    pieces = []
    for member in range(group_ratio):
        pieces.append(from_root(green_panel, "col", lax.axis_index("row") * group_ratio + member))
    rows_block = jnp.concatenate(pieces, axis=2).reshape(freq_count, 2 * span_i, local_pts)
    cols_block = green_panel.reshape(freq_count, 2 * span_j, local_pts)

    def run_sweep(sweep_idx, log_field):
        whole_log = lax.all_gather(log_field, ("row", "col"), axis=1, tiled=True)
        psd_field = jnp.exp(whole_log)
        weighted = (green_panel * psd_field[:, None, None, :]).astype(jnp.bfloat16)
        weighted = weighted.reshape(freq_count, 2 * span_j, local_pts)
        partial_value = correlate(rows_block, weighted)
        pair_sum = pair_total(partial_value)
        adjoint = (pair_scale * (quad_weight * pair_sum - observed)).astype(jnp.bfloat16)
        point_part = point_terms(adjoint, cols_block, rows_block, psd_field, quad_weight)
        gradient = lax.psum_scatter(point_part, ("row", "col"), scatter_dimension=1, tiled=True)
        return descend(log_field, gradient, entry_count)

    log_final = lax.fori_loop(0, ITERS, run_sweep, log_start)
    return log_final[None]


def solution(mesh):
    return jax.shard_map(
        body,
        mesh=mesh,
        in_specs=(
            P(None, None, "col", "pts"),
            P("pts", None, ("row", "col")),
            P(None, None, "row", "col"),
            P("row", "col"),
        ),
        out_specs=P("pts", None, ("row", "col")),
        check_vma=False,
    )
```

profile of v0, /device:TPU:1, one launch (start us, length us, event | category | flops | bytes accessed | tf_op | source)
XLA Modules:
  0.0 2389.3 jit_solution(17483855640603249323)
XLA Ops:
  6.5 0.0 all-reduce.6.cloned.1.call-start
  6.5 3.3 broadcast_select_fusion.1
  9.9 0.0 copy-start.3
  9.9 0.0 copy-start.4
  9.9 0.0 all-reduce.6.cloned.1.call-update
  9.9 0.9 copy-done.3
  10.8 0.7 copy.12
  11.4 0.0 copy-done.4
  11.4 141.9 %all-reduce.6.cloned.1.call-done = (bf16[4,2,32,3072]{3,2,1,0:T(8,128)(2,1)}, bf16[4,2,32,3072]{3,2,1,0:T(8,128)(2,1)}) async-done(((bf16[4,2,32,3072]{3,2,1,0:T(8,128)(2,1)}, bf16[4,2,32,3072]{3,2,1,0:T(8,128)(2,1)}), (bf16[4,2,32,3072]{3,2,1,0:T(8,128)(2,1)}, bf16[4,2,32,3072]{3,2,1,0:T(8,128)(2,1)})) %all-reduce.6.cloned.1.call-update) | async-done | bytes 3145744 | tf_op jit(solution)/shard_map/psum | solution.py:15
  153.4 0.0 copy-start.2
  153.4 0.0 copy-start.5
  153.4 2.1 pad_maximum_fusion.1
  155.5 0.0 copy-done.2
  155.5 0.0 copy-done.5
  155.5 2226.4 %while.10 = (s32[]{:T(128)}, f32[4,24]{1,0:T(4,128)S(1)}, bf16[4,128,3072]{2,1,0:T(8,128)(2,1)S(1)}, f32[64,32]{0,1:T(8,128)S(1)}, bf16[4,2,32,3072]{3,2,1,0:T(8...) while((s32[]{:T(128)}, f32[4,24]{1,0:T(4,128)S(1)}, ...), condition=%wide.region_8.9_spmd, body=%wide.region_2.8_spmd.sunk | while | flops 410173920 | bytes 11200641 | solution.py:80
  155.5 289.3 %all-gather.2 = f32[128,24,4]{1,2,0:T(4,128)S(1)} all-gather(f32[1,24,4]{1,2,0:T(4,128)S(1)} %bitcast.56), channel_id=1, replica_groups=mesh['row'=8,'col'=16,'pts'=2] {'row','col'}, dimensions={0}, use_global_device_ids=true | all-gather | bytes 49536 | tf_op jit(solution)/shard_map/while/body/eval_jaxpr/all_gather | solution.py:69
  444.8 0.1 copy.17
  445.0 0.1 copy.18
  445.1 0.2 reshape.22
  445.3 0.0 copy-start
  445.3 2.6 fusion.33
  447.9 0.1 fusion.34
  448.1 69.0 %psum.32 = bf16[4,2,64,32]{2,3,0,1:T(8,128)(2,1)S(1)} all-reduce(bf16[4,2,64,32]{2,3,0,1:T(8,128)(2,1)S(1)} %pad_maximum_fusion.3), channel_id=1, replica_groups=mesh['row'=8,'col'=16,'pts'=2] {'pts'}, use_global_device_ids=true, to_apply=%region_3.3 | all-reduce | flops 16384 | bytes 65536 | tf_op jit(solution)/shard_map/while/body/eval_jaxpr/psum | solution.py:19
  517.1 0.0 copy-done
  517.2 2.5 multiply_reduce_fusion.4
  519.7 571.1 %all-reduce.3 = f32[4,3072]{1,0:T(4,128)S(1)} all-reduce(f32[4,3072]{1,0:T(4,128)S(1)} %multiply_multiply_fusion.2), channel_id=2, replica_groups=mesh['row'=8,'col'=16,'pts'=2] {'row','col'}, use_global_device_ids=true, to_apply=%region_5.5.clone | all-reduce | flops 12288 | bytes 98304 | tf_op jit(solution)/shard_map/while
  1090.8 0.7 dynamic-slice.9
  1092.2 0.8 multiply_reduce_fusion.5
  1092.9 181.0 %psum.33 = f32[]{:T(128)} all-reduce(f32[]{:T(128)} %multiply_reduce_fusion.5), channel_id=1, replica_groups=mesh['row'=8,'col'=16,'pts'=2] {'row','col','pts'}, use_global_device_ids=true, to_apply=%region_7.7 | all-reduce | flops 1 | bytes 8 | tf_op jit(solution)/shard_map/while/body/eval_jaxpr/psum | solution.py:23
  1274.7 0.1 divide_subtract_fusion.2
  1274.8 287.2 %all-gather.2 = f32[128,24,4]{1,2,0:T(4,128)S(1)} all-gather(f32[1,24,4]{1,2,0:T(4,128)S(1)} %bitcast.56), channel_id=1, replica_groups=mesh['row'=8,'col'=16,'pts'=2] {'row','col'}, dimensions={0}, use_global_device_ids=true | all-gather | bytes 49536 | tf_op jit(solution)/shard_map/while/body/eval_jaxpr/all_gather | solution.py:69
  1562.0 0.1 copy.17
  1562.2 0.1 copy.18
  1562.3 0.2 reshape.22
  1562.5 0.0 copy-start
  1562.5 2.6 fusion.33
  1565.1 0.1 fusion.34
  1565.3 58.9 %psum.32 = bf16[4,2,64,32]{2,3,0,1:T(8,128)(2,1)S(1)} all-reduce(bf16[4,2,64,32]{2,3,0,1:T(8,128)(2,1)S(1)} %pad_maximum_fusion.3), channel_id=1, replica_groups=mesh['row'=8,'col'=16,'pts'=2] {'pts'}, use_global_device_ids=true, to_apply=%region_3.3 | all-reduce | flops 16384 | bytes 65536 | tf_op jit(solution)/shard_map/while/body/eval_jaxpr/psum | solution.py:19
  1624.1 0.0 copy-done
  1624.2 2.5 multiply_reduce_fusion.4
  1626.8 571.1 %all-reduce.3 = f32[4,3072]{1,0:T(4,128)S(1)} all-reduce(f32[4,3072]{1,0:T(4,128)S(1)} %multiply_multiply_fusion.2), channel_id=2, replica_groups=mesh['row'=8,'col'=16,'pts'=2] {'row','col'}, use_global_device_ids=true, to_apply=%region_5.5.clone | all-reduce | flops 12288 | bytes 98304 | tf_op jit(solution)/shard_map/while
  2197.9 0.7 dynamic-slice.9
  2199.3 0.8 multiply_reduce_fusion.5
  2200.0 181.0 %psum.33 = f32[]{:T(128)} all-reduce(f32[]{:T(128)} %multiply_reduce_fusion.5), channel_id=1, replica_groups=mesh['row'=8,'col'=16,'pts'=2] {'row','col','pts'}, use_global_device_ids=true, to_apply=%region_7.7 | all-reduce | flops 1 | bytes 8 | tf_op jit(solution)/shard_map/while/body/eval_jaxpr/psum | solution.py:23
  2381.8 0.1 divide_subtract_fusion.2
  2381.9 0.0 copy-start.1
  2381.9 0.6 copy-done.1
  (13 shorter events, 0.2 us)
Async XLA Ops:
  6.5 146.8 %all-reduce.6.cloned.1.call-start = ((), (), s32[]{:S(2)}) async-start(), calls=%async_computation | async-start | bytes 6291456 | tf_op jit(solution)/shard_map/psum | solution.py:15
  9.9 0.9 copy-start.3
  9.9 1.6 copy-start.4
  153.4 2.1 copy-start.2
  153.4 2.1 copy-start.5
  445.3 71.8 %copy-start = (f32[4,2,64,32]{2,3,0,1:T(8,128)S(1)}, f32[4,2,64,32]{2,3,0,1:T(8,128)}, u32[]{:S(2)}) copy-start(f32[4,2,64,32]{2,3,0,1:T(8,128)} %get-tuple-element.175) | copy-start | bytes 196612 | tf_op jit(solution)/shard_map/while
  1562.5 61.7 %copy-start = (f32[4,2,64,32]{2,3,0,1:T(8,128)S(1)}, f32[4,2,64,32]{2,3,0,1:T(8,128)}, u32[]{:S(2)}) copy-start(f32[4,2,64,32]{2,3,0,1:T(8,128)} %get-tuple-element.175) | copy-start | bytes 196612 | tf_op jit(solution)/shard_map/while
  2381.9 0.6 copy-start.1
Sparse Core Ops, SparseCore 0:
  10.1 143.2 all-reduce.5
where the time goes:
time: 2390 us
  blocking collectives  2210 us (92%)
  waiting for transfers between devices  142 us (6%)
    while x2, blocking collectives  1140 us
    all_gather x2, blocking collectives, run_sweep(): whole_log = lax.all_gather(log_field, ('row', 'col'), axis=1, tiled=True)  577 us
    psum x2, blocking collectives, descend(): squares = lax.psum(jnp.sum(gradient * gradient), ('row', 'col', 'pts'))  362 us
    psum x1, waiting for transfers between devices, from_root(): return lax.psum(block, axis)  142 us
    psum x2, blocking collectives, pair_total(): lax.psum(partial_value.astype(jnp.bfloat16), 'pts').astype(jnp.float32)  128 us
  transfers between devices with their start and end apart: 1, of which 1 were waited for; matrix products, arithmetic and copies ran while one was open for 0% of the time, Pallas kernels for 0%

commit v1 on v0

v1 whole, which is shorter than its diff:
```python
import functools

import jax
import jax.numpy as jnp
from jax import lax
from jax.experimental import pallas as pl
from jax.experimental.pallas import tpu as pltpu
from jax.sharding import PartitionSpec as P

MESH = pl.DeviceIdType.MESH
HIGHEST = lax.Precision.HIGHEST
F32 = jnp.float32
BF16 = jnp.bfloat16

ITERS = 2
NX = 4
NZ = 8
NO = 8
ST = 32
NP = 768
RUN = 24
ENTRIES = 4 * 6144
QUAD = 1.0 / 6144
EPSILON = 1e-06
DESCENT = 0.1

FIRST_J = (0, 1, 2)


def wait_bytes(ref, sem):
    pltpu.make_async_copy(ref, ref, sem).wait()


def kernel(
    green, logp, obs, weights, out,
    u, y, x_left, obs_v, w_v, msg, e_in, d_all, w_all,
    l_src, l_in, l_z, l_rows, c_part, rs, b_out, b_full, g_mine, g_all, s_mine, s_all, t_mine, t_all,
    m_mine, o_mine, m_in, o_in, rows_m, rows_g,
    in_sem, gr_sem, gs_sem, er_sem, es_sem, lr_sem, ls_sem, ls2_sem,
    ph_r, ph_s, mr_sem, ms_sem, or_sem, os_sem,
):
    row = lax.axis_index("row")
    col = lax.axis_index("col")
    core = lax.axis_index("pts")
    yh, x = row // 4, row % 4
    yl, z = col // 8, col % 8
    me = yh * 4 + yl * 2 + core
    other = 1 - yl

    def dev(x_, yh_, yl_, z_, core_):
        return (yh_ * 4 + x_, yl_ * 8 + z_, core_)

    def zdev(d):
        return dev(x, yh, yl, (z + d) % NZ, core)

    def odev(d):
        o = (me + d) % NO
        return o, dev(x, o // 4, (o // 2) % 2, z, o % 2)

    def xdev(d):
        return dev((x + d) % NX, yh, yl, z, core)

    def is_me(dest):
        return jnp.logical_and(jnp.logical_and(dest[0] == row, dest[1] == col), dest[2] == core)

    obs_copy = pltpu.make_async_copy(obs, obs_v, in_sem.at[0])
    w_copy = pltpu.make_async_copy(weights, w_v, in_sem.at[1])
    obs_copy.start()
    w_copy.start()

    def panel(comp, lo):
        start = pl.multiple_of((yh * 2 + lo) * NP, 128)
        return green.at[x, comp, :, pl.ds(start, NP)]

    for comp in range(2):
        pltpu.make_async_copy(panel(comp, yl), u.at[yl, 0, 0, :, pl.ds(comp * NP, NP)], in_sem.at[2]).start()

    def centre(zi, zj):
        delta = (zj - zi) % NZ
        from_i = jnp.where(delta >= 4, 2, jnp.where(delta >= 2, 1, 0))
        from_j = jnp.where(delta == 7, 0, 1)
        zc = jnp.where(delta <= 4, zi + from_i, zj + from_j) % NZ
        return delta, zc

    def pair_dest(plane, zl):
        delta, zc = centre(2 * x + zl, z)
        swap = delta >= 5
        return delta, dev(plane, jnp.where(swap, yl, yh), jnp.where(swap, yh, yl), zc, core)

    pair_dests = []
    for plane in range(NX):
        for zl in range(2):
            pair_dests.append((plane, zl) + pair_dest(plane, zl))
    offsets = ((0, 0), (0, 1), (-1, 1), (-1, 2), (-2, 2), (2, -1), (1, -1), (1, 0))
    pair_sources = []
    for delta in range(NZ):
        zi, zj = (z + offsets[delta][0]) % NZ, (z + offsets[delta][1]) % NZ
        if delta <= 4:
            pair_sources.append(dev(zi // 2, yh, yl, zj, core))
        else:
            pair_sources.append(dev(zi // 2, yl, yh, zj, core))

    up = [dev(plane, yh, x // 2, z, core) for plane in range(NX)]
    down = [dev(2 * yl + k // 2, yh, k % 2, z, core) for k in range(4)]

    barrier = pltpu.get_barrier_semaphore()
    expected = jnp.int32(7 + 7 + 3 + 16)
    for d in range(1, NZ):
        pl.semaphore_signal(barrier, inc=1, device_id=zdev(d), device_id_type=MESH)
    for d in range(1, NO):
        pl.semaphore_signal(barrier, inc=1, device_id=odev(d)[1], device_id_type=MESH)
    for d in range(1, NX):
        pl.semaphore_signal(barrier, inc=1, device_id=xdev(d), device_id_type=MESH)
    for dest in pair_sources + up + down:
        @pl.when(jnp.logical_not(is_me(dest)))
        def _(dest=dest):
            pl.semaphore_signal(barrier, inc=1, device_id=dest, device_id_type=MESH)
    for dest in [entry[3] for entry in pair_dests] + up + down:
        expected = expected - is_me(dest).astype(jnp.int32)
    pl.semaphore_wait(barrier, expected)

    def send(src, dst, s_sem, r_sem, dest):
        copy = pltpu.make_async_remote_copy(
            src_ref=src, dst_ref=dst, send_sem=s_sem, recv_sem=r_sem, device_id=dest, device_id_type=MESH
        )
        copy.start()
        return copy

    partner = dev(x, yh, other, z, core)
    lane = lambda comp: pl.ds(comp * NP, NP)
    for comp in range(2):
        send(panel(comp, other), u.at[yl, 0, 0, :, lane(comp)], gs_sem.at[0], gr_sem.at[0], partner)
    for comp in range(2):
        send(panel(comp, yl), x_left.at[1, yl, :, lane(comp)], gs_sem.at[1], gr_sem.at[1], zdev(1))
        send(panel(comp, yl), u.at[yl, 1, 0, :, lane(comp)], gs_sem.at[2], gr_sem.at[2], zdev(-1))

    def send_or_keep(src, dst, s_sem, r_sem, dest):
        mine = is_me(dest)
        @pl.when(jnp.logical_not(mine))
        def _():
            send(src, dst, s_sem, r_sem, dest)
        @pl.when(mine)
        def _():
            pltpu.make_async_copy(src, dst, r_sem).start()

    def finish_send(src, s_sem, dest):
        @pl.when(jnp.logical_not(is_me(dest)))
        def _():
            wait_bytes(src, s_sem)

    slot = (x % 2) * 2 + yl
    l_src[...] = jnp.zeros_like(l_src)
    for f in range(NX):
        l_src[f, :, 0:RUN] = logp[0, f : f + 1, :]
    for f in range(NX):
        send_or_keep(l_src.at[f], l_in.at[slot], ls_sem.at[f], lr_sem.at[0], up[f])

    obs_copy.wait()
    w_copy.wait()
    for zl in range(2):
        w = w_v[zl * ST : (zl + 1) * ST, :].astype(F32)
        for f in range(NX):
            real = w * obs_v[f, 0, zl * ST : (zl + 1) * ST, :]
            imag = w * obs_v[f, 1, zl * ST : (zl + 1) * ST, :]
            msg[f, zl] = jnp.concatenate([real, imag, w, w], axis=1)

    wait_bytes(l_in, lr_sem.at[0])
    for d in range(1, NZ):
        send(l_in, l_z.at[z], ls2_sem.at[0], lr_sem.at[1], zdev(d))
    l_z[z] = l_in[...]

    for k, (plane, zl, delta, dest) in enumerate(pair_dests):
        send_or_keep(msg.at[plane, zl], e_in.at[delta], es_sem.at[k], er_sem.at[0], dest)

    wait_bytes(u.at[other, 0, 0], gr_sem.at[0])
    send(u.at[other, 0, 0], x_left.at[1, other], gs_sem.at[3], gr_sem.at[3], zdev(1))
    send(u.at[other, 0, 0], u.at[other, 1, 0], gs_sem.at[4], gr_sem.at[4], zdev(-1))

    wait_bytes(l_z.at[pl.ds(0, NZ - 1)], lr_sem.at[1])
    for zz in range(NZ):
        for k in range(4):
            l_rows[k * NZ + zz : k * NZ + zz + 1, :] = l_z[zz, k]
    point = lax.broadcasted_iota(jnp.int32, (128, NP), 1)
    run_of = lax.shift_right_logical(point * 2731, 16)
    spread = (point - run_of * RUN == lax.broadcasted_iota(jnp.int32, (128, NP), 0)).astype(F32)
    spread_rows = jnp.dot(l_rows[...], spread, precision=HIGHEST, preferred_element_type=F32)
    run_row = lax.shift_right_logical(lax.broadcasted_iota(jnp.int32, (32, NP), 1) * 2731, 16)
    log_field = jnp.sum(
        jnp.where(run_row == lax.broadcasted_iota(jnp.int32, (32, NP), 0), spread_rows, 0.0), axis=0, keepdims=True
    )

    def build_turned(lo, j):
        u[lo, j, 1, :, 0:NP] = -u[lo, j, 0, :, NP : 2 * NP]
        u[lo, j, 1, :, NP : 2 * NP] = u[lo, j, 0, :, 0:NP]

    def build_weighted(j, psd2):
        for lo in range(2):
            for turn in range(2):
                y[lo, j, turn] = (u[lo, j, turn].astype(F32) * psd2).astype(BF16)

    def correlate(g):
        count = 2 if g < 2 else 1
        left = x_left[g].reshape(2 * ST, 2 * NP)
        for lo in range(2):
            right = y[lo, FIRST_J[g] : FIRST_J[g] + count].reshape(count * 2 * ST, 2 * NP)
            product = lax.dot_general(left, right, (((1,), (1,)), ((), ())), preferred_element_type=F32)
            if count == 1:
                product = jnp.concatenate([product, jnp.zeros_like(product)], axis=1)
            c_part[lo, g] = product.reshape(2, 2, 16, 128).astype(BF16)

    psd = jnp.exp(log_field)
    psd2 = jnp.concatenate([psd, psd], axis=1)

    wait_bytes(u.at[yl, 0, 0], in_sem.at[2])
    for lo in range(2):
        x_left[0, lo] = u[lo, 0, 0]
        build_turned(lo, 0)
    build_weighted(0, psd2)

    for half, at in ((yl, 1), (other, 3)):
        wait_bytes(x_left.at[1, half], gr_sem.at[at])
        send(x_left.at[1, half], x_left.at[2, half], gs_sem.at[at + 4], gr_sem.at[at + 4], zdev(1))
        wait_bytes(u.at[half, 1, 0], gr_sem.at[at + 1])
        send(u.at[half, 1, 0], u.at[half, 2, 0], gs_sem.at[at + 5], gr_sem.at[at + 5], zdev(-1))
    for lo in range(2):
        build_turned(lo, 1)
    build_weighted(1, psd2)
    correlate(0)

    wait_bytes(e_in, er_sem.at[0])
    lane_at = lax.broadcasted_iota(jnp.int32, (ST, 128), 1)
    same = (lane_at % ST == lax.broadcasted_iota(jnp.int32, (ST, 128), 0)).astype(F32)
    part_at = lane_at // ST

    def turned(block):
        full = lax.dot_general(block, same, (((0,), (0,)), ((), ())), precision=HIGHEST, preferred_element_type=F32)
        result = jnp.where(part_at == 0, full[0:ST], 0.0)
        result = jnp.where(part_at == 1, -full[ST : 2 * ST], result)
        result = jnp.where(part_at == 2, full[2 * ST : 3 * ST], result)
        return jnp.where(part_at == 3, full[3 * ST : 4 * ST], result)

    none = jnp.zeros((ST, 128), F32)
    slots = (
        (e_in[0], e_in[1] + turned(e_in[7])),
        (e_in[2] + turned(e_in[6]), e_in[3] + turned(e_in[5])),
        (e_in[4], none),
    )
    low = lane_at < 2 * ST
    for g, (first, second) in enumerate(slots):
        d_all[g] = jnp.where(low, first, pltpu.roll(second, 64, 1))
        w_all[g] = jnp.where(low, pltpu.roll(first, 64, 1), second) * QUAD

    for half, at in ((yl, 5), (other, 7)):
        wait_bytes(x_left.at[2, half], gr_sem.at[at])
        wait_bytes(u.at[half, 2, 0], gr_sem.at[at + 1])
    for lo in range(2):
        build_turned(lo, 2)
    build_weighted(2, psd2)
    correlate(1)
    correlate(2)

    def exchange_rest(it, psd):
        phase = lambda k: (ph_s.at[it, k], ph_r.at[it, k])
        s_sem, r_sem = phase(0)
        for d in range(1, NO):
            o, dest = odev(d)
            send(c_part.at[(o // 2) % 2, :, o // 4, o % 2], rs.at[it, d - 1], s_sem, r_sem, dest)
        total = c_part[yl, :, yh, core].astype(F32)
        wait_bytes(rs.at[it], r_sem)
        for d in range(NO - 1):
            total = total + rs[it, d].astype(F32)
        own_rows = pl.ds(pl.multiple_of(core * 16, 16), 16)
        b_out[it] = (w_all[:, own_rows, :] * total - d_all[:, own_rows, :]).astype(BF16)
        s_sem, r_sem = phase(1)
        for d in range(1, NO):
            send(b_out.at[it], b_full.at[it, yl, :, yh, core], s_sem, r_sem, odev(d)[1])
        b_full[it, yl, :, yh, core] = b_out[it]
        wait_bytes(rs.at[it], r_sem)

        width = 384
        terms = []
        for c in range(2 * NP // width):
            lanes = slice(c * width, (c + 1) * width)
            term = jnp.zeros((1, width), F32)
            for g in range(3):
                count = 2 if g < 2 else 1
                field = jnp.zeros((2 * ST, width), F32)
                for lo in range(2):
                    b = b_full[it, lo, g].reshape(2 * ST, 128)[:, 0 : count * 2 * ST]
                    right = u[lo, FIRST_J[g] : FIRST_J[g] + count, :, :, lanes].reshape(count * 2 * ST, width)
                    field = field + jnp.dot(b, right, preferred_element_type=F32)
                left = x_left[g, :, :, lanes].reshape(2 * ST, width).astype(F32)
                term = term + jnp.sum(left * field, axis=0, keepdims=True)
            terms.append(term)
        half = len(terms) // 2
        mine = jnp.concatenate([terms[k] + terms[half + k] for k in range(half)], axis=1)
        g_mine[it] = mine
        s_sem, r_sem = phase(2)
        for d in range(1, NZ):
            send(g_mine.at[it], g_all.at[it, z], s_sem, r_sem, zdev(d))
        g_all[it, z] = mine
        wait_bytes(g_all.at[it, pl.ds(0, NZ - 1)], r_sem)
        summed = g_all[it, 0]
        for k in range(1, NZ):
            summed = summed + g_all[it, k]
        return QUAD * psd * summed

    def root_mean(it, gradient):
        phase = lambda k: (ph_s.at[it, k], ph_r.at[it, k])
        squares = jnp.broadcast_to(jnp.sum(gradient * gradient, axis=1, keepdims=True), (1, 128))
        s_mine[it] = squares
        s_sem, r_sem = phase(3)
        for d in range(1, NO):
            send(s_mine.at[it], s_all.at[it, me], s_sem, r_sem, odev(d)[1])
        s_all[it, me] = squares
        wait_bytes(s_all.at[it, pl.ds(0, NO - 1)], r_sem)
        total = s_all[it, 0]
        for k in range(1, NO):
            total = total + s_all[it, k]
        t_mine[it] = total
        s_sem, r_sem = phase(4)
        for d in range(1, NX):
            send(t_mine.at[it], t_all.at[it, x], s_sem, r_sem, xdev(d))
        t_all[it, x] = total
        wait_bytes(t_all.at[it, pl.ds(0, NX - 1)], r_sem)
        total = t_all[it, 0]
        for k in range(1, NX):
            total = total + t_all[it, k]
        return jnp.sqrt(total / ENTRIES + EPSILON)[:, 0:1]

    gradient = exchange_rest(0, psd)
    log_field = log_field - DESCENT * gradient / root_mean(0, gradient)

    psd = jnp.exp(log_field)
    psd2 = jnp.concatenate([psd, psd], axis=1)
    for j in range(3):
        build_weighted(j, psd2)
    for g in range(3):
        correlate_wait = g == 0
        if correlate_wait:
            wait_bytes(rs.at[0], ph_s.at[0, 0])
        correlate(g)
    m_mine[...] = log_field
    for k in range(4):
        send_or_keep(m_mine, m_in.at[x], ms_sem.at[k], mr_sem.at[0], down[k])
    gradient = exchange_rest(1, psd)
    o_mine[...] = gradient
    for k in range(4):
        send_or_keep(o_mine, o_in.at[x], os_sem.at[k], or_sem.at[0], down[k])
    scale = root_mean(1, gradient)

    wait_bytes(m_in, mr_sem.at[0])
    wait_bytes(o_in, or_sem.at[0])
    rows_m[...] = jnp.zeros_like(rows_m)
    for f in range(NX):
        rows_m[f : f + 1, :] = m_in[f] - DESCENT * o_in[f] / scale
    start = (slot * NZ + z) * RUN
    pick = (
        lax.broadcasted_iota(jnp.int32, (NP, 128), 0) == lax.broadcasted_iota(jnp.int32, (NP, 128), 1) + start
    ).astype(F32)
    picked = jnp.dot(rows_m[...], pick, precision=HIGHEST, preferred_element_type=F32)
    out[0] = picked[0:NX, 0:RUN]

    for k in range(9):
        wait_bytes(x_left.at[1, 0], gs_sem.at[k])
    for f in range(NX):
        finish_send(l_src.at[f], ls_sem.at[f], up[f])
    wait_bytes(l_z.at[pl.ds(0, NZ - 1)], ls2_sem.at[0])
    for k, (plane, zl, delta, dest) in enumerate(pair_dests):
        finish_send(msg.at[plane, zl], es_sem.at[k], dest)
    for it in range(ITERS):
        if it > 0:
            wait_bytes(rs.at[it], ph_s.at[it, 0])
        wait_bytes(rs.at[it], ph_s.at[it, 1])
        wait_bytes(g_all.at[it, pl.ds(0, NZ - 1)], ph_s.at[it, 2])
        wait_bytes(s_all.at[it, pl.ds(0, NO - 1)], ph_s.at[it, 3])
        wait_bytes(t_all.at[it, pl.ds(0, NX - 1)], ph_s.at[it, 4])
    for k in range(4):
        finish_send(m_mine, ms_sem.at[k], down[k])
        finish_send(o_mine, os_sem.at[k], down[k])


def body(green_panel, log_psd, observed, pair_weights):
    vmem = pltpu.VMEM
    dma = pltpu.SemaphoreType.DMA
    return pl.pallas_call(
        kernel,
        out_shape=jax.ShapeDtypeStruct(log_psd.shape, F32),
        in_specs=[
            pl.BlockSpec(memory_space=pl.ANY),
            pl.BlockSpec(memory_space=pltpu.VMEM),
            pl.BlockSpec(memory_space=pl.ANY),
            pl.BlockSpec(memory_space=pl.ANY),
        ],
        out_specs=pl.BlockSpec(memory_space=pltpu.VMEM),
        scratch_shapes=[
            vmem((2, 3, 2, ST, 2 * NP), BF16),
            vmem((2, 3, 2, ST, 2 * NP), BF16),
            vmem((3, 2, ST, 2 * NP), BF16),
            vmem((4, 2, 64, ST), F32),
            vmem((64, ST), jnp.int32),
            vmem((NX, 2, ST, 128), F32),
            vmem((NZ, ST, 128), F32),
            vmem((3, ST, 128), F32),
            vmem((3, ST, 128), F32),
            vmem((NX, 1, 128), F32),
            vmem((4, 1, 128), F32),
            vmem((NZ, 4, 1, 128), F32),
            vmem((32, 128), F32),
            vmem((2, 3, 2, 2, 16, 128), BF16),
            vmem((ITERS, NO - 1, 3, 16, 128), BF16),
            vmem((ITERS, 3, 16, 128), BF16),
            vmem((ITERS, 2, 3, 2, 2, 16, 128), BF16),
            vmem((ITERS, 1, NP), F32),
            vmem((ITERS, NZ, 1, NP), F32),
            vmem((ITERS, 1, 128), F32),
            vmem((ITERS, NO, 1, 128), F32),
            vmem((ITERS, 1, 128), F32),
            vmem((ITERS, NX, 1, 128), F32),
            vmem((1, NP), F32),
            vmem((1, NP), F32),
            vmem((NX, 1, NP), F32),
            vmem((NX, 1, NP), F32),
            vmem((8, NP), F32),
            vmem((8, NP), F32),
            dma((3,)),
            dma((9,)),
            dma((9,)),
            dma((1,)),
            dma((8,)),
            dma((2,)),
            dma((4,)),
            dma((1,)),
            dma((ITERS, 5)),
            dma((ITERS, 5)),
            dma((1,)),
            dma((4,)),
            dma((1,)),
            dma((4,)),
        ],
        compiler_params=pltpu.CompilerParams(
            collective_id=0, has_side_effects=True, vmem_limit_bytes=40 * 1024 * 1024
        ),
    )(green_panel, log_psd, observed, pair_weights)


def solution(mesh):
    return jax.shard_map(
        body,
        mesh=mesh,
        in_specs=(
            P(None, None, "col", "pts"),
            P("pts", None, ("row", "col")),
            P(None, None, "row", "col"),
            P("row", "col"),
        ),
        out_specs=P("pts", None, ("row", "col")),
        check_vma=False,
    )
```

time: 2390 us -> 72.2 us (0.03)
  blocking collectives: 2210 us -> 0 us
  waiting for transfers between devices: 142 us -> 0 us
  Pallas kernels: 0 us -> 67.5 us
    while x2 -> x0, blocking collectives: 1140 us -> none
    all_gather x2 -> x0, blocking collectives: 577 us -> none  [run_sweep(): whole_log = lax.all_gather(log_field, ('row', 'col'), axis=1, tiled=True)]
    psum x4 -> x0, blocking collectives: 490 us -> none  [the longest x2 362 us: descend(): squares = lax.psum(jnp.sum(gradient * gradient), ('row', 'col', 'pts'))]
    psum x1 -> x0, waiting for transfers between devices: 142 us -> none  [from_root(): return lax.psum(block, axis)]
    pallas_call x0 -> x1, Pallas kernels: none -> 67.5 us  [body(): pl.pallas_call(kernel, out_shape=jax.ShapeDtypeStruct(log_psd.shape, F32)...]
  transfers between devices with their start and end apart: 1 -> 0, of which waited for: 1 -> 0; matrix products, arithmetic and copies ran while one was open for 0% -> 0% of each run, Pallas kernels for 0% -> 0%
where the time goes in v1:
time: 72.2 us; the launch traced here: 72 us
  Pallas kernels  67.5 us (93%)
  local copies, waits for them, and re-layouts  4.5 us (6%)
    pallas_call x1, Pallas kernels, body(): pl.pallas_call(kernel, out_shape=jax.ShapeDtypeStruct(log_psd.shape, F32)...  67.5 us
    unnamed x7, local copies, waits for them, and re-layouts  4.5 us

profile of v1, /device:TPU:1, one launch (start us, length us, event | category | flops | bytes accessed | tf_op | source)
XLA Modules:
  0.0 72.0 jit_solution(3170341251486842188)
XLA Ops:
  0.0 0.8 %copy.6.weights = s32[64,32]{1,0:T(8,128)S(1)} copy(s32[64,32]{0,1:T(8,128)} %param.7) | data formatting | bytes 16384 | tf_op args[3]
  0.8 1.0 %copy.5.obs = f32[4,2,64,32]{3,2,1,0:T(8,128)S(1)} copy(f32[4,2,64,32]{2,3,1,0:T(8,128)} %param.6) | data formatting | bytes 131072 | tf_op args[2]
  1.8 0.0 copy-start
  1.9 1.4 %copy-done = bf16[4,2,32,3072]{3,2,1,0:T(8,128)(2,1)S(1)} copy-done((bf16[4,2,32,3072]{3,2,1,0:T(8,128)(2,1)S(1)}, bf16[4,2,32,3072]{3,2,1,0:T(8,128)(2,1)}, u32[]{:S(2)}) %copy-start) | copy-done | bytes 1572888
  3.3 0.0 copy-start.1
  3.3 0.7 copy-done.1
  3.9 67.5 %shard_map.46 = f32[1,4,24]{2,1,0:T(4,128)S(1)} custom-call(bf16[4,2,32,3072]{3,2,1,0:T(8,128)(2,1)S(1)} %copy-done, f32[1,4,24]{2,1,0:T(4,128)S(1)} %copy-done.1, f32[4,2,64,32]{3,2,1,0:T(8,128)S(1)} %copy.5.obs, s32[64,32]{1,0:T(8,128)S(1)} %copy.6.weights), custom_call_target="tpu_custom_call" | custom-call | tf_op jit(solution)/shard_map/pallas_call | solution.py:386
  71.4 0.6 copy.8
Async XLA Ops:
  1.8 1.4 %copy-start = (bf16[4,2,32,3072]{3,2,1,0:T(8,128)(2,1)S(1)}, bf16[4,2,32,3072]{3,2,1,0:T(8,128)(2,1)}, u32[]{:S(2)}) copy-start(bf16[4,2,32,3072]{3,2,1,0:T(8,128)(2,1)} %green.1) | copy-start | bytes 4718596
  3.3 0.7 copy-start.1

commit v2 on v1

v2 whole, which is shorter than its diff:
```python
import functools

import jax
import jax.numpy as jnp
from jax import lax
from jax.experimental import pallas as pl
from jax.experimental.pallas import tpu as pltpu
from jax.sharding import PartitionSpec as P

MESH = pl.DeviceIdType.MESH
HIGHEST = lax.Precision.HIGHEST
F32 = jnp.float32
BF16 = jnp.bfloat16

ITERS = 2
NX = 4
NZ = 8
NO = 8
NS = NX * NO
ST = 32
NP = 768
RUN = 24
ENTRIES = 4 * 6144
QUAD = 1.0 / 6144
EPSILON = 1e-06
DESCENT = 0.1

FIRST_J = (0, 1, 2)


def wait_bytes(ref, sem):
    pltpu.make_async_copy(ref, ref, sem).wait()


def kernel(
    green, logp, obs, weights, out,
    u, x_left, x_psd, log_v, obs_v, w_v, msg, e_in, d_all, w_all,
    l_src, l_in, l_z, l_rows, c_part, rs, b_out, b_full, g_mine, g_all, s_mine, s_all,
    m_mine, o_mine, m_in, o_in, rows_m, rows_o,
    in_sem, gr_sem, gs_sem, er_sem, es_sem, lr_sem, ls_sem, ls2_sem,
    ph_r, ph_s, mr_sem, ms_sem, or_sem, os_sem,
):
    row = lax.axis_index("row")
    col = lax.axis_index("col")
    core = lax.axis_index("pts")
    yh, x = row // 4, row % 4
    yl, z = col // 8, col % 8
    me = yh * 4 + yl * 2 + core
    other = 1 - yl

    def dev(x_, yh_, yl_, z_, core_):
        return (yh_ * 4 + x_, yl_ * 8 + z_, core_)

    def zdev(d):
        return dev(x, yh, yl, (z + d) % NZ, core)

    def odev(d):
        o = (me + d) % NO
        return o, dev(x, o // 4, (o // 2) % 2, z, o % 2)

    def sdev(d):
        r = (x * NO + me + d) % NS
        return dev(r // NO, (r // 4) % 2, (r // 2) % 2, z, r % 2)

    def is_me(dest):
        return jnp.logical_and(jnp.logical_and(dest[0] == row, dest[1] == col), dest[2] == core)

    obs_copy = pltpu.make_async_copy(obs, obs_v, in_sem.at[0])
    w_copy = pltpu.make_async_copy(weights, w_v, in_sem.at[1])
    log_copy = pltpu.make_async_copy(logp, log_v, in_sem.at[3])
    log_copy.start()
    obs_copy.start()
    w_copy.start()

    def panel(comp, lo):
        start = pl.multiple_of((yh * 2 + lo) * NP, 128)
        return green.at[x, comp, :, pl.ds(start, NP)]

    for comp in range(2):
        pltpu.make_async_copy(panel(comp, yl), u.at[yl, 0, 0, :, pl.ds(comp * NP, NP)], in_sem.at[2]).start()

    def centre(zi, zj):
        delta = (zj - zi) % NZ
        from_i = jnp.where(delta >= 2, 1, 0)
        from_j = jnp.where(delta == 7, 0, jnp.where(delta == 4, 2, 1))
        zc = jnp.where(delta <= 3, zi + from_i, zj + from_j) % NZ
        return delta, zc

    def pair_dest(plane, zl):
        delta, zc = centre(2 * x + zl, z)
        swap = jnp.logical_or(delta == 0, delta >= 4)
        return delta, dev(plane, jnp.where(swap, yl, yh), jnp.where(swap, yh, yl), zc, core)

    pair_dests = []
    for plane in range(NX):
        for zl in range(2):
            pair_dests.append((plane, zl) + pair_dest(plane, zl))
    offsets = ((0, 0), (0, 1), (-1, 1), (-1, 2), (2, -2), (2, -1), (1, -1), (1, 0))
    pair_sources = []
    for delta in range(NZ):
        zi, zj = (z + offsets[delta][0]) % NZ, (z + offsets[delta][1]) % NZ
        if 1 <= delta <= 3:
            pair_sources.append(dev(zi // 2, yh, yl, zj, core))
        else:
            pair_sources.append(dev(zi // 2, yl, yh, zj, core))

    up = [dev(plane, yh, x // 2, z, core) for plane in range(NX)]
    down = [dev(2 * yl + k // 2, yh, k % 2, z, core) for k in range(4)]

    barrier = pltpu.get_barrier_semaphore()
    expected = jnp.int32(NZ - 1 + NS - 1 + 16)
    for d in range(1, NZ):
        pl.semaphore_signal(barrier, inc=1, device_id=zdev(d), device_id_type=MESH)
    for d in range(1, NS):
        pl.semaphore_signal(barrier, inc=1, device_id=sdev(d), device_id_type=MESH)
    for dest in pair_sources + up + down:
        @pl.when(jnp.logical_not(is_me(dest)))
        def _(dest=dest):
            pl.semaphore_signal(barrier, inc=1, device_id=dest, device_id_type=MESH)
    for dest in [entry[3] for entry in pair_dests] + up + down:
        expected = expected - is_me(dest).astype(jnp.int32)
    pl.semaphore_wait(barrier, expected)

    def send(src, dst, s_sem, r_sem, dest):
        copy = pltpu.make_async_remote_copy(
            src_ref=src, dst_ref=dst, send_sem=s_sem, recv_sem=r_sem, device_id=dest, device_id_type=MESH
        )
        copy.start()
        return copy

    partner = dev(x, yh, other, z, core)
    lane = lambda comp: pl.ds(comp * NP, NP)
    for comp in range(2):
        send(panel(comp, other), u.at[yl, 0, 0, :, lane(comp)], gs_sem.at[0], gr_sem.at[0], partner)
    for comp in range(2):
        send(panel(comp, yl), x_left.at[1, yl, :, lane(comp)], gs_sem.at[1], gr_sem.at[1], zdev(1))
        send(panel(comp, yl), u.at[yl, 1, 0, :, lane(comp)], gs_sem.at[2], gr_sem.at[2], zdev(-1))

    def send_or_keep(src, dst, s_sem, r_sem, dest):
        mine = is_me(dest)
        @pl.when(jnp.logical_not(mine))
        def _():
            send(src, dst, s_sem, r_sem, dest)
        @pl.when(mine)
        def _():
            pltpu.make_async_copy(src, dst, r_sem).start()

    def finish_send(src, s_sem, dest):
        @pl.when(jnp.logical_not(is_me(dest)))
        def _():
            wait_bytes(src, s_sem)

    slot = (x % 2) * 2 + yl
    l_src[...] = jnp.zeros_like(l_src)
    log_copy.wait()
    for f in range(NX):
        l_src[f, :, 0:RUN] = log_v[0, f : f + 1, :]
    for f in range(NX):
        send_or_keep(l_src.at[f], l_in.at[slot], ls_sem.at[f], lr_sem.at[0], up[f])

    wait_bytes(u.at[other, 0, 0], gr_sem.at[0])
    send(u.at[other, 0, 0], x_left.at[1, other], gs_sem.at[3], gr_sem.at[3], zdev(1))
    send(u.at[other, 0, 0], u.at[other, 1, 0], gs_sem.at[4], gr_sem.at[4], zdev(-1))

    wait_bytes(l_in, lr_sem.at[0])
    for d in range(1, NZ):
        send(l_in, l_z.at[z], ls2_sem.at[0], lr_sem.at[1], zdev(d))
    l_z[z] = l_in[...]

    def build_turned(lo, j):
        u[lo, j, 1, :, 0:NP] = -u[lo, j, 0, :, NP : 2 * NP]
        u[lo, j, 1, :, NP : 2 * NP] = u[lo, j, 0, :, 0:NP]

    def build_weighted(g, psd2):
        for lo in range(2):
            x_psd[g, lo] = (x_left[g, lo].astype(F32) * psd2).astype(BF16)

    def correlate(g):
        count = 2 if g < 2 else 1
        left = x_psd[g].reshape(2 * ST, 2 * NP)
        for lo in range(2):
            right = u[lo, FIRST_J[g] : FIRST_J[g] + count].reshape(count * 2 * ST, 2 * NP)
            product = lax.dot_general(left, right, (((1,), (1,)), ((), ())), preferred_element_type=F32)
            if count == 1:
                product = jnp.concatenate([product, jnp.zeros_like(product)], axis=1)
            c_part[lo, g] = product.reshape(2, 2, 16, 128).astype(BF16)

    def pass_on(half, at):
        wait_bytes(x_left.at[1, half], gr_sem.at[at])
        send(x_left.at[1, half], x_left.at[2, half], gs_sem.at[at + 4], gr_sem.at[at + 4], zdev(1))
        wait_bytes(u.at[half, 1, 0], gr_sem.at[at + 1])
        send(u.at[half, 1, 0], u.at[half, 2, 0], gs_sem.at[at + 5], gr_sem.at[at + 5], zdev(-1))

    obs_copy.wait()
    w_copy.wait()
    for zl in range(2):
        w = w_v[:, zl * ST : (zl + 1) * ST].astype(F32)
        for f in range(NX):
            real = w * obs_v[f, 0, :, zl * ST : (zl + 1) * ST]
            imag = w * obs_v[f, 1, :, zl * ST : (zl + 1) * ST]
            msg[f, zl] = jnp.concatenate([real, imag, w, w], axis=1)

    wait_bytes(u.at[yl, 0, 0], in_sem.at[2])
    for lo in range(2):
        x_left[0, lo] = u[lo, 0, 0]
        build_turned(lo, 0)
    pass_on(yl, 1)

    wait_bytes(l_z.at[pl.ds(0, NZ - 1)], lr_sem.at[1])
    for zz in range(NZ):
        for k in range(4):
            l_rows[k * NZ + zz : k * NZ + zz + 1, :] = l_z[zz, k]
    point = lax.broadcasted_iota(jnp.int32, (128, NP), 1)
    run_of = lax.shift_right_logical(point * 2731, 16)
    spread = (point - run_of * RUN == lax.broadcasted_iota(jnp.int32, (128, NP), 0)).astype(F32)
    spread_rows = jnp.dot(l_rows[...], spread, precision=HIGHEST, preferred_element_type=F32)
    run_row = lax.shift_right_logical(lax.broadcasted_iota(jnp.int32, (32, NP), 1) * 2731, 16)
    log_field = jnp.sum(
        jnp.where(run_row == lax.broadcasted_iota(jnp.int32, (32, NP), 0), spread_rows, 0.0), axis=0, keepdims=True
    )
    psd = jnp.exp(log_field)
    psd2 = jnp.concatenate([psd, psd], axis=1)
    build_weighted(0, psd2)

    pass_on(other, 3)
    for k, (plane, zl, delta, dest) in enumerate(pair_dests):
        send_or_keep(msg.at[plane, zl], e_in.at[delta], es_sem.at[k], er_sem.at[0], dest)
    for lo in range(2):
        build_turned(lo, 1)
    build_weighted(1, psd2)
    correlate(0)

    for half, at in ((yl, 5), (other, 7)):
        wait_bytes(x_left.at[2, half], gr_sem.at[at])
        wait_bytes(u.at[half, 2, 0], gr_sem.at[at + 1])
    for lo in range(2):
        build_turned(lo, 2)
    build_weighted(2, psd2)
    correlate(1)
    correlate(2)

    def pair_terms():
        wait_bytes(e_in, er_sem.at[0])
        lane_at = lax.broadcasted_iota(jnp.int32, (ST, 128), 1)
        same = (lane_at % ST == lax.broadcasted_iota(jnp.int32, (ST, 128), 0)).astype(F32)
        part_at = lane_at // ST

        def turned(block):
            full = lax.dot_general(block, same, (((0,), (0,)), ((), ())), precision=HIGHEST, preferred_element_type=F32)
            result = jnp.where(part_at == 0, full[0:ST], full[ST : 2 * ST])
            result = jnp.where(part_at == 2, full[2 * ST : 3 * ST], result)
            return jnp.where(part_at == 3, full[3 * ST : 4 * ST], result)

        def conj(block):
            return jnp.where(part_at == 1, -block, block)

        slots = (
            (conj(e_in[0]), turned(e_in[1]) + conj(e_in[7])),
            (turned(e_in[2]) + conj(e_in[6]), turned(e_in[3]) + conj(e_in[5])),
            (conj(e_in[4]), jnp.zeros((ST, 128), F32)),
        )
        low = lane_at < 2 * ST
        for g, (first, second) in enumerate(slots):
            d_all[g] = jnp.where(low, first, pltpu.roll(second, 64, 1))
            w_all[g] = jnp.where(low, pltpu.roll(first, 64, 1), second) * QUAD

    def exchange_rest(it, psd):
        phase = lambda k: (ph_s.at[it, k], ph_r.at[it, k])
        s_sem, r_sem = phase(0)
        for d in range(1, NO):
            o, dest = odev(d)
            send(c_part.at[(o // 2) % 2, :, o // 4, o % 2], rs.at[it, d - 1], s_sem, r_sem, dest)
        total = c_part[yl, :, yh, core].astype(F32)
        if it == 0:
            pair_terms()
        wait_bytes(rs.at[it], r_sem)
        for d in range(NO - 1):
            total = total + rs[it, d].astype(F32)
        own_rows = pl.ds(pl.multiple_of(core * 16, 16), 16)
        b_out[it] = (w_all[:, own_rows, :] * total - d_all[:, own_rows, :]).astype(BF16)
        s_sem, r_sem = phase(1)
        for d in range(1, NO):
            send(b_out.at[it], b_full.at[it, yl, :, yh, core], s_sem, r_sem, odev(d)[1])
        b_full[it, yl, :, yh, core] = b_out[it]
        wait_bytes(rs.at[it], r_sem)

        width = 384
        terms = []
        for c in range(2 * NP // width):
            lanes = slice(c * width, (c + 1) * width)
            term = jnp.zeros((1, width), F32)
            for g in range(3):
                count = 2 if g < 2 else 1
                field = jnp.zeros((2 * ST, width), F32)
                for lo in range(2):
                    b = b_full[it, lo, g].reshape(2 * ST, 128)[:, 0 : count * 2 * ST]
                    right = u[lo, FIRST_J[g] : FIRST_J[g] + count, :, :, lanes].reshape(count * 2 * ST, width)
                    field = field + jnp.dot(b, right, preferred_element_type=F32)
                left = x_left[g, :, :, lanes].reshape(2 * ST, width).astype(F32)
                term = term + jnp.sum(left * field, axis=0, keepdims=True)
            terms.append(term)
        half = len(terms) // 2
        mine = jnp.concatenate([terms[k] + terms[half + k] for k in range(half)], axis=1)
        g_mine[it] = mine
        s_sem, r_sem = phase(2)
        for d in range(1, NZ):
            send(g_mine.at[it], g_all.at[it, z], s_sem, r_sem, zdev(d))
        g_all[it, z] = mine
        wait_bytes(g_all.at[it, pl.ds(0, NZ - 1)], r_sem)
        summed = g_all[it, 0]
        for k in range(1, NZ):
            summed = summed + g_all[it, k]
        return QUAD * psd * summed

    def start_mean(it, gradient):
        squares = jnp.broadcast_to(jnp.sum(gradient * gradient, axis=1, keepdims=True), (1, 128))
        s_mine[it] = squares
        for d in range(1, NS):
            send(s_mine.at[it], s_all.at[it, x * NO + me], ph_s.at[it, 3], ph_r.at[it, 3], sdev(d))
        s_all[it, x * NO + me] = squares

    def finish_mean(it):
        wait_bytes(s_all.at[it, pl.ds(0, NS - 1)], ph_r.at[it, 3])
        total = jnp.sum(s_all[it], axis=0)
        return jnp.sqrt(total / ENTRIES + EPSILON)[:, 0:1]

    gradient = exchange_rest(0, psd)
    start_mean(0, gradient)
    wait_bytes(rs.at[0], ph_s.at[0, 0])
    log_field = log_field - DESCENT * gradient / finish_mean(0)

    psd = jnp.exp(log_field)
    psd2 = jnp.concatenate([psd, psd], axis=1)
    for g in range(3):
        build_weighted(g, psd2)
        correlate(g)
    m_mine[...] = log_field
    for k in range(4):
        send_or_keep(m_mine, m_in.at[x], ms_sem.at[k], mr_sem.at[0], down[k])
    gradient = exchange_rest(1, psd)
    start_mean(1, gradient)
    o_mine[...] = gradient
    for k in range(4):
        send_or_keep(o_mine, o_in.at[x], os_sem.at[k], or_sem.at[0], down[k])

    start = (slot * NZ + z) * RUN
    pick = (
        lax.broadcasted_iota(jnp.int32, (NP, 128), 0) == lax.broadcasted_iota(jnp.int32, (NP, 128), 1) + start
    ).astype(F32)

    def run_of_points(rows, parts):
        rows[...] = jnp.zeros_like(rows)
        for f in range(NX):
            rows[f : f + 1, :] = parts[f]
        return jnp.dot(rows[...], pick, precision=HIGHEST, preferred_element_type=F32)[0:NX, 0:RUN]

    wait_bytes(m_in, mr_sem.at[0])
    own_field = run_of_points(rows_m, m_in)
    wait_bytes(o_in, or_sem.at[0])
    own_gradient = run_of_points(rows_o, o_in)
    out[0] = own_field - DESCENT * own_gradient / finish_mean(1)

    for k in range(9):
        wait_bytes(x_left.at[1, 0], gs_sem.at[k])
    for f in range(NX):
        finish_send(l_src.at[f], ls_sem.at[f], up[f])
    wait_bytes(l_z.at[pl.ds(0, NZ - 1)], ls2_sem.at[0])
    for k, (plane, zl, delta, dest) in enumerate(pair_dests):
        finish_send(msg.at[plane, zl], es_sem.at[k], dest)
    for it in range(ITERS):
        if it > 0:
            wait_bytes(rs.at[it], ph_s.at[it, 0])
        wait_bytes(rs.at[it], ph_s.at[it, 1])
        wait_bytes(g_all.at[it, pl.ds(0, NZ - 1)], ph_s.at[it, 2])
        wait_bytes(s_all.at[it, pl.ds(0, NS - 1)], ph_s.at[it, 3])
    for k in range(4):
        finish_send(m_mine, ms_sem.at[k], down[k])
        finish_send(o_mine, os_sem.at[k], down[k])


def body(green_panel, log_psd, observed, pair_weights):
    vmem = pltpu.VMEM
    dma = pltpu.SemaphoreType.DMA
    return pl.pallas_call(
        kernel,
        out_shape=jax.ShapeDtypeStruct(log_psd.shape, F32),
        in_specs=[
            pl.BlockSpec(memory_space=pltpu.HBM),
            pl.BlockSpec(memory_space=pltpu.HBM),
            pl.BlockSpec(memory_space=pltpu.HBM),
            pl.BlockSpec(memory_space=pltpu.HBM),
        ],
        out_specs=pl.BlockSpec(memory_space=pltpu.VMEM),
        scratch_shapes=[
            vmem((2, 3, 2, ST, 2 * NP), BF16),
            vmem((3, 2, ST, 2 * NP), BF16),
            vmem((3, 2, ST, 2 * NP), BF16),
            vmem((1, NX, RUN), F32),
            vmem((NX, 2, ST, 2 * ST), F32),
            vmem((ST, 2 * ST), jnp.int32),
            vmem((NX, 2, ST, 128), F32),
            vmem((NZ, ST, 128), F32),
            vmem((3, ST, 128), F32),
            vmem((3, ST, 128), F32),
            vmem((NX, 1, 128), F32),
            vmem((4, 1, 128), F32),
            vmem((NZ, 4, 1, 128), F32),
            vmem((32, 128), F32),
            vmem((2, 3, 2, 2, 16, 128), BF16),
            vmem((ITERS, NO - 1, 3, 16, 128), BF16),
            vmem((ITERS, 3, 16, 128), BF16),
            vmem((ITERS, 2, 3, 2, 2, 16, 128), BF16),
            vmem((ITERS, 1, NP), F32),
            vmem((ITERS, NZ, 1, NP), F32),
            vmem((ITERS, 1, 128), F32),
            vmem((ITERS, NS, 1, 128), F32),
            vmem((1, NP), F32),
            vmem((1, NP), F32),
            vmem((NX, 1, NP), F32),
            vmem((NX, 1, NP), F32),
            vmem((8, NP), F32),
            vmem((8, NP), F32),
            dma((4,)),
            dma((9,)),
            dma((9,)),
            dma((1,)),
            dma((8,)),
            dma((2,)),
            dma((4,)),
            dma((1,)),
            dma((ITERS, 4)),
            dma((ITERS, 4)),
            dma((1,)),
            dma((4,)),
            dma((1,)),
            dma((4,)),
        ],
        compiler_params=pltpu.CompilerParams(
            collective_id=0, has_side_effects=True, vmem_limit_bytes=63 * 1024 * 1024
        ),
    )(green_panel, log_psd, jnp.swapaxes(observed, 2, 3), pair_weights.T)


def solution(mesh):
    return jax.shard_map(
        body,
        mesh=mesh,
        in_specs=(
            P(None, None, "col", "pts"),
            P("pts", None, ("row", "col")),
            P(None, None, "row", "col"),
            P("row", "col"),
        ),
        out_specs=P("pts", None, ("row", "col")),
        check_vma=False,
    )
```

time: 72.2 us -> 65.3 us (0.904)
  Pallas kernels: 67.5 us -> 63.9 us
  local copies, waits for them, and re-layouts: 4.5 us -> 1.26 us
    pallas_call x1, Pallas kernels: 67.5 us -> 63.9 us  [body(): pl.pallas_call(kernel, out_shape=jax.ShapeDtypeStruct(log_psd.shape, F32)...]
    unnamed x7 -> x1, local copies, waits for them, and re-layouts: 4.5 us -> 1.26 us
where the time goes in v2:
time: 65.3 us; the launch traced here: 65.2 us
  Pallas kernels  63.9 us (98%)
  local copies, waits for them, and re-layouts  1.26 us (2%)
    pallas_call x1, Pallas kernels, body(): pl.pallas_call(kernel, out_shape=jax.ShapeDtypeStruct(log_psd.shape, F32)...  63.9 us

profile of v2, /device:TPU:1, one launch (start us, length us, event | category | flops | bytes accessed | tf_op | source)
XLA Modules:
  0.0 65.2 jit_solution(15033303239492567678)
XLA Ops:
  0.0 63.9 %shard_map.46 = f32[1,4,24]{2,1,0:T(4,128)} custom-call(bf16[4,2,32,3072]{3,2,1,0:T(8,128)(2,1)} %green.1, f32[1,4,24]{2,1,0:T(4,128)} %logp.1, f32[4,2,32,64]{3,2,1,0:T(8,128)} %bitcast.2, s32[32,64]{1,0:T(8,128)} %bitcast.3), custom_call_target="tpu_custom_call" | custom-call | tf_op jit(solution)/shard_map/pallas_call | solution.py:384
  64.0 1.3 %copy.6 = f32[1,4,24]{2,1,0:T(4,128)} copy(f32[1,4,24]{2,1,0:T(4,128)} %shard_map.46) | data formatting | bytes 768

commit v3 on v2

--- a/solution.py
+++ b/solution.py
@@ -45,22 +45,28 @@
     core = lax.axis_index("pts")
     yh, x = row // 4, row % 4
     yl, z = col // 8, col % 8
-    me = yh * 4 + yl * 2 + core
+    mine_at = x * NO + yh * 4 + yl * 2 + core
     other = 1 - yl
 
     def dev(x_, yh_, yl_, z_, core_):
         return (yh_ * 4 + x_, yl_ * 8 + z_, core_)
 
+    z_steps = (4, 3, 5, 2, 6, 1, 7)
+    y_at = yh * 2 + yl
+    o_steps = [(dy, dc) for dy in (2, 1, 3, 0) for dc in (1, 0) if dy or dc]
+    s_steps = [(dx, dy, dc) for dx in (2, 1, 3, 0) for dy in (2, 1, 3, 0) for dc in (1, 0) if dx or dy or dc]
+    s_steps.sort(key=lambda step: -min(step[0], 4 - step[0]) - min(step[1], 4 - step[1]) - 0.5 * step[2])
+
     def zdev(d):
         return dev(x, yh, yl, (z + d) % NZ, core)
 
-    def odev(d):
-        o = (me + d) % NO
-        return o, dev(x, o // 4, (o // 2) % 2, z, o % 2)
-
-    def sdev(d):
-        r = (x * NO + me + d) % NS
-        return dev(r // NO, (r // 4) % 2, (r // 2) % 2, z, r % 2)
+    def odev(dy, dc):
+        to_y, to_core = (y_at + dy) % 4, (core + dc) % 2
+        return to_y, to_core, dev(x, to_y // 2, to_y % 2, z, to_core)
+
+    def sdev(dx, dy, dc):
+        to_y = (y_at + dy) % 4
+        return dev((x + dx) % NX, to_y // 2, to_y % 2, z, (core + dc) % 2)
 
     def is_me(dest):
         return jnp.logical_and(jnp.logical_and(dest[0] == row, dest[1] == col), dest[2] == core)
@@ -107,18 +113,35 @@
     up = [dev(plane, yh, x // 2, z, core) for plane in range(NX)]
     down = [dev(2 * yl + k // 2, yh, k % 2, z, core) for k in range(4)]
 
+    log_copy.wait()
+    l_src[...] = jnp.zeros_like(l_src)
+    for f in range(NX):
+        l_src[f, :, 0:RUN] = log_v[0, f : f + 1, :]
+
+    partner = dev(x, yh, other, z, core)
+    diagonal = {d: dev(x, yh, other, (z + d) % NZ, core) for d in (1, -1)}
     barrier = pltpu.get_barrier_semaphore()
-    expected = jnp.int32(NZ - 1 + NS - 1 + 16)
-    for d in range(1, NZ):
+    expected = jnp.int32(NZ - 1 + NO - 1 + 2 + 8)
+    for dest in (partner, zdev(1), zdev(-1), diagonal[1], diagonal[-1]):
+        pl.semaphore_signal(barrier, inc=1, device_id=dest, device_id_type=MESH)
+    for d in z_steps[:-2]:
         pl.semaphore_signal(barrier, inc=1, device_id=zdev(d), device_id_type=MESH)
-    for d in range(1, NS):
-        pl.semaphore_signal(barrier, inc=1, device_id=sdev(d), device_id_type=MESH)
-    for dest in pair_sources + up + down:
+    for step in o_steps:
+        pl.semaphore_signal(barrier, inc=1, device_id=odev(*step)[2], device_id_type=MESH)
+    expected = expected + 1
+    for dest in up + down:
         @pl.when(jnp.logical_not(is_me(dest)))
         def _(dest=dest):
             pl.semaphore_signal(barrier, inc=1, device_id=dest, device_id_type=MESH)
-    for dest in [entry[3] for entry in pair_dests] + up + down:
         expected = expected - is_me(dest).astype(jnp.int32)
+    for delta, source in enumerate(pair_sources):
+        if not 1 <= delta <= 3:
+            @pl.when(jnp.logical_not(is_me(source)))
+            def _(source=source):
+                pl.semaphore_signal(barrier, inc=1, device_id=source, device_id_type=MESH)
+    for plane, zl, delta, dest in pair_dests:
+        swap = jnp.logical_or(delta == 0, delta >= 4)
+        expected = expected + jnp.logical_and(swap, jnp.logical_not(is_me(dest))).astype(jnp.int32)
     pl.semaphore_wait(barrier, expected)
 
     def send(src, dst, s_sem, r_sem, dest):
@@ -128,13 +151,7 @@
         copy.start()
         return copy
 
-    partner = dev(x, yh, other, z, core)
-    lane = lambda comp: pl.ds(comp * NP, NP)
-    for comp in range(2):
-        send(panel(comp, other), u.at[yl, 0, 0, :, lane(comp)], gs_sem.at[0], gr_sem.at[0], partner)
-    for comp in range(2):
-        send(panel(comp, yl), x_left.at[1, yl, :, lane(comp)], gs_sem.at[1], gr_sem.at[1], zdev(1))
-        send(panel(comp, yl), u.at[yl, 1, 0, :, lane(comp)], gs_sem.at[2], gr_sem.at[2], zdev(-1))
+    lanes_of = [pl.ds(comp * NP, NP) for comp in range(2)]
 
     def send_or_keep(src, dst, s_sem, r_sem, dest):
         mine = is_me(dest)
@@ -151,21 +168,19 @@
             wait_bytes(src, s_sem)
 
     slot = (x % 2) * 2 + yl
-    l_src[...] = jnp.zeros_like(l_src)
-    log_copy.wait()
-    for f in range(NX):
-        l_src[f, :, 0:RUN] = log_v[0, f : f + 1, :]
     for f in range(NX):
         send_or_keep(l_src.at[f], l_in.at[slot], ls_sem.at[f], lr_sem.at[0], up[f])
 
-    wait_bytes(u.at[other, 0, 0], gr_sem.at[0])
-    send(u.at[other, 0, 0], x_left.at[1, other], gs_sem.at[3], gr_sem.at[3], zdev(1))
-    send(u.at[other, 0, 0], u.at[other, 1, 0], gs_sem.at[4], gr_sem.at[4], zdev(-1))
-
-    wait_bytes(l_in, lr_sem.at[0])
-    for d in range(1, NZ):
-        send(l_in, l_z.at[z], ls2_sem.at[0], lr_sem.at[1], zdev(d))
-    l_z[z] = l_in[...]
+    def launch(k, comp, src, dst, dest):
+        send(src, dst.at[:, lanes_of[comp]], gs_sem.at[comp, k], gr_sem.at[comp, k], dest)
+
+    for comp in range(2):
+        launch(1, comp, panel(comp, yl), x_left.at[1, yl], zdev(1))
+        launch(2, comp, panel(comp, yl), u.at[yl, 1, 0], zdev(-1))
+        launch(0, comp, panel(comp, other), u.at[yl, 0, 0], partner)
+    for comp in range(2):
+        launch(3, comp, panel(comp, other), x_left.at[1, yl], diagonal[1])
+        launch(4, comp, panel(comp, other), u.at[yl, 1, 0], diagonal[-1])
 
     def build_turned(lo, j):
         u[lo, j, 1, :, 0:NP] = -u[lo, j, 0, :, NP : 2 * NP]
@@ -185,11 +200,17 @@
                 product = jnp.concatenate([product, jnp.zeros_like(product)], axis=1)
             c_part[lo, g] = product.reshape(2, 2, 16, 128).astype(BF16)
 
+    def arrive(k, comp, dst):
+        wait_bytes(dst.at[:, lanes_of[comp]], gr_sem.at[comp, k])
+
     def pass_on(half, at):
-        wait_bytes(x_left.at[1, half], gr_sem.at[at])
-        send(x_left.at[1, half], x_left.at[2, half], gs_sem.at[at + 4], gr_sem.at[at + 4], zdev(1))
-        wait_bytes(u.at[half, 1, 0], gr_sem.at[at + 1])
-        send(u.at[half, 1, 0], u.at[half, 2, 0], gs_sem.at[at + 5], gr_sem.at[at + 5], zdev(-1))
+        for comp in range(2):
+            piece = x_left.at[1, half]
+            arrive(at, comp, piece)
+            launch(at + 4, comp, piece.at[:, lanes_of[comp]], x_left.at[2, half], zdev(1))
+            piece = u.at[half, 1, 0]
+            arrive(at + 1, comp, piece)
+            launch(at + 5, comp, piece.at[:, lanes_of[comp]], u.at[half, 2, 0], zdev(-1))
 
     obs_copy.wait()
     w_copy.wait()
@@ -200,13 +221,23 @@
             imag = w * obs_v[f, 1, :, zl * ST : (zl + 1) * ST]
             msg[f, zl] = jnp.concatenate([real, imag, w, w], axis=1)
 
+    wait_bytes(l_in, lr_sem.at[0])
+    for d in z_steps:
+        send(l_in, l_z.at[z], ls2_sem.at[0], lr_sem.at[1], zdev(d))
+    l_z[z] = l_in[...]
+    pass_on(yl, 1)
     wait_bytes(u.at[yl, 0, 0], in_sem.at[2])
+    pass_on(other, 3)
+    wait_bytes(l_z.at[pl.ds(0, NZ - 1)], lr_sem.at[1])
+    for k, (plane, zl, delta, dest) in enumerate(pair_dests):
+        send_or_keep(msg.at[plane, zl], e_in.at[delta], es_sem.at[k], er_sem.at[0], dest)
+    for comp in range(2):
+        arrive(0, comp, u.at[other, 0, 0])
     for lo in range(2):
         x_left[0, lo] = u[lo, 0, 0]
         build_turned(lo, 0)
-    pass_on(yl, 1)
-
-    wait_bytes(l_z.at[pl.ds(0, NZ - 1)], lr_sem.at[1])
+        build_turned(lo, 1)
+
     for zz in range(NZ):
         for k in range(4):
             l_rows[k * NZ + zz : k * NZ + zz + 1, :] = l_z[zz, k]
@@ -222,17 +253,13 @@
     psd2 = jnp.concatenate([psd, psd], axis=1)
     build_weighted(0, psd2)
 
-    pass_on(other, 3)
-    for k, (plane, zl, delta, dest) in enumerate(pair_dests):
-        send_or_keep(msg.at[plane, zl], e_in.at[delta], es_sem.at[k], er_sem.at[0], dest)
-    for lo in range(2):
-        build_turned(lo, 1)
     build_weighted(1, psd2)
     correlate(0)
 
     for half, at in ((yl, 5), (other, 7)):
-        wait_bytes(x_left.at[2, half], gr_sem.at[at])
-        wait_bytes(u.at[half, 2, 0], gr_sem.at[at + 1])
+        for comp in range(2):
+            arrive(at, comp, x_left.at[2, half])
+            arrive(at + 1, comp, u.at[half, 2, 0])
     for lo in range(2):
         build_turned(lo, 2)
     build_weighted(2, psd2)
@@ -264,24 +291,43 @@
             d_all[g] = jnp.where(low, first, pltpu.roll(second, 64, 1))
             w_all[g] = jnp.where(low, pltpu.roll(first, 64, 1), second) * QUAD
 
+    def finish_phase(it, phase):
+        sizes = (rs.at[it], rs.at[it], g_all.at[it, pl.ds(0, NZ - 1)], s_all.at[it, pl.ds(0, NS - 1)])
+        wait_bytes(sizes[phase], ph_s.at[it, phase])
+
+    def finish_start():
+        for comp in range(2):
+            for k in range(9):
+                wait_bytes(x_left.at[1, 0, :, lanes_of[comp]], gs_sem.at[comp, k])
+        for f in range(NX):
+            finish_send(l_src.at[f], ls_sem.at[f], up[f])
+        wait_bytes(l_z.at[pl.ds(0, NZ - 1)], ls2_sem.at[0])
+        for k, (plane, zl, delta, dest) in enumerate(pair_dests):
+            finish_send(msg.at[plane, zl], es_sem.at[k], dest)
+        for phase in range(1, 4):
+            finish_phase(0, phase)
+
     def exchange_rest(it, psd):
         phase = lambda k: (ph_s.at[it, k], ph_r.at[it, k])
         s_sem, r_sem = phase(0)
-        for d in range(1, NO):
-            o, dest = odev(d)
-            send(c_part.at[(o // 2) % 2, :, o // 4, o % 2], rs.at[it, d - 1], s_sem, r_sem, dest)
+        for k, step in enumerate(o_steps):
+            to_y, to_core, dest = odev(*step)
+            send(c_part.at[to_y % 2, :, to_y // 2, to_core], rs.at[it, k], s_sem, r_sem, dest)
         total = c_part[yl, :, yh, core].astype(F32)
         if it == 0:
             pair_terms()
+        else:
+            finish_start()
         wait_bytes(rs.at[it], r_sem)
         for d in range(NO - 1):
             total = total + rs[it, d].astype(F32)
         own_rows = pl.ds(pl.multiple_of(core * 16, 16), 16)
         b_out[it] = (w_all[:, own_rows, :] * total - d_all[:, own_rows, :]).astype(BF16)
         s_sem, r_sem = phase(1)
-        for d in range(1, NO):
-            send(b_out.at[it], b_full.at[it, yl, :, yh, core], s_sem, r_sem, odev(d)[1])
+        for step in o_steps:
+            send(b_out.at[it], b_full.at[it, yl, :, yh, core], s_sem, r_sem, odev(*step)[2])
         b_full[it, yl, :, yh, core] = b_out[it]
+        finish_phase(it, 0)
         wait_bytes(rs.at[it], r_sem)
 
         width = 384
@@ -303,7 +349,7 @@
         mine = jnp.concatenate([terms[k] + terms[half + k] for k in range(half)], axis=1)
         g_mine[it] = mine
         s_sem, r_sem = phase(2)
-        for d in range(1, NZ):
+        for d in z_steps:
             send(g_mine.at[it], g_all.at[it, z], s_sem, r_sem, zdev(d))
         g_all[it, z] = mine
         wait_bytes(g_all.at[it, pl.ds(0, NZ - 1)], r_sem)
@@ -315,9 +361,9 @@
     def start_mean(it, gradient):
         squares = jnp.broadcast_to(jnp.sum(gradient * gradient, axis=1, keepdims=True), (1, 128))
         s_mine[it] = squares
-        for d in range(1, NS):
-            send(s_mine.at[it], s_all.at[it, x * NO + me], ph_s.at[it, 3], ph_r.at[it, 3], sdev(d))
-        s_all[it, x * NO + me] = squares
+        for step in s_steps:
+            send(s_mine.at[it], s_all.at[it, mine_at], ph_s.at[it, 3], ph_r.at[it, 3], sdev(*step))
+        s_all[it, mine_at] = squares
 
     def finish_mean(it):
         wait_bytes(s_all.at[it, pl.ds(0, NS - 1)], ph_r.at[it, 3])
@@ -326,7 +372,6 @@
 
     gradient = exchange_rest(0, psd)
     start_mean(0, gradient)
-    wait_bytes(rs.at[0], ph_s.at[0, 0])
     log_field = log_field - DESCENT * gradient / finish_mean(0)
 
     psd = jnp.exp(log_field)
@@ -360,19 +405,9 @@
     own_gradient = run_of_points(rows_o, o_in)
     out[0] = own_field - DESCENT * own_gradient / finish_mean(1)
 
-    for k in range(9):
-        wait_bytes(x_left.at[1, 0], gs_sem.at[k])
-    for f in range(NX):
-        finish_send(l_src.at[f], ls_sem.at[f], up[f])
-    wait_bytes(l_z.at[pl.ds(0, NZ - 1)], ls2_sem.at[0])
-    for k, (plane, zl, delta, dest) in enumerate(pair_dests):
-        finish_send(msg.at[plane, zl], es_sem.at[k], dest)
-    for it in range(ITERS):
-        if it > 0:
-            wait_bytes(rs.at[it], ph_s.at[it, 0])
-        wait_bytes(rs.at[it], ph_s.at[it, 1])
-        wait_bytes(g_all.at[it, pl.ds(0, NZ - 1)], ph_s.at[it, 2])
-        wait_bytes(s_all.at[it, pl.ds(0, NS - 1)], ph_s.at[it, 3])
+    finish_phase(1, 1)
+    finish_phase(1, 2)
+    finish_phase(1, 3)
     for k in range(4):
         finish_send(m_mine, ms_sem.at[k], down[k])
         finish_send(o_mine, os_sem.at[k], down[k])
@@ -421,8 +456,8 @@
             vmem((8, NP), F32),
             vmem((8, NP), F32),
             dma((4,)),
-            dma((9,)),
-            dma((9,)),
+            dma((2, 9)),
+            dma((2, 9)),
             dma((1,)),
             dma((8,)),
             dma((2,)),

time: 65.3 us -> 61.8 us (0.946)
  Pallas kernels: 63.9 us -> 60.4 us
    pallas_call x1, Pallas kernels: 63.9 us -> 60.4 us  [body(): pl.pallas_call(kernel, out_shape=jax.ShapeDtypeStruct(log_psd.shape, F32)...]
where the time goes in v3:
time: 61.8 us; the launch traced here: 61.7 us
  Pallas kernels  60.4 us (98%)
  local copies, waits for them, and re-layouts  1.26 us (2%)
    pallas_call x1, Pallas kernels, body(): pl.pallas_call(kernel, out_shape=jax.ShapeDtypeStruct(log_psd.shape, F32)...  60.4 us
    unnamed x1, local copies, waits for them, and re-layouts  1.26 us

profile of v3, /device:TPU:1, one launch (start us, length us, event | category | flops | bytes accessed | tf_op | source)
XLA Modules:
  0.0 61.7 jit_solution(2672320498653287167)
XLA Ops:
  0.0 60.4 %shard_map.46 = f32[1,4,24]{2,1,0:T(4,128)} custom-call(bf16[4,2,32,3072]{3,2,1,0:T(8,128)(2,1)} %green.1, f32[1,4,24]{2,1,0:T(4,128)} %logp.1, f32[4,2,32,64]{3,2,1,0:T(8,128)} %bitcast.2, s32[32,64]{1,0:T(8,128)} %bitcast.3), custom_call_target="tpu_custom_call" | custom-call | tf_op jit(solution)/shard_map/pallas_call | solution.py:419
  60.5 1.3 %copy.6 = f32[1,4,24]{2,1,0:T(4,128)} copy(f32[1,4,24]{2,1,0:T(4,128)} %shard_map.46) | data formatting | bytes 768

commit v4 on v3

--- a/solution.py
+++ b/solution.py
@@ -34,11 +34,11 @@
 
 def kernel(
     green, logp, obs, weights, out,
-    u, x_left, x_psd, log_v, obs_v, w_v, msg, e_in, d_all, w_all,
+    u, x_left, x_psd, away, log_v, obs_v, w_v, msg, e_in, d_all, w_all,
     l_src, l_in, l_z, l_rows, c_part, rs, b_out, b_full, g_mine, g_all, s_mine, s_all,
     m_mine, o_mine, m_in, o_in, rows_m, rows_o,
     in_sem, gr_sem, gs_sem, er_sem, es_sem, lr_sem, ls_sem, ls2_sem,
-    ph_r, ph_s, mr_sem, ms_sem, or_sem, os_sem,
+    tokens, ph_r, ph_s, mr_sem, ms_sem, or_sem, os_sem,
 ):
     row = lax.axis_index("row")
     col = lax.axis_index("col")
@@ -82,8 +82,13 @@
         start = pl.multiple_of((yh * 2 + lo) * NP, 128)
         return green.at[x, comp, :, pl.ds(start, NP)]
 
+    lanes_of = [pl.ds(comp * NP, NP) for comp in range(2)]
+    staged = []
     for comp in range(2):
-        pltpu.make_async_copy(panel(comp, yl), u.at[yl, 0, 0, :, pl.ds(comp * NP, NP)], in_sem.at[2]).start()
+        staged.append(pltpu.make_async_copy(panel(comp, yl), u.at[yl, 0, 0, :, lanes_of[comp]], in_sem.at[4 + comp]))
+        staged.append(pltpu.make_async_copy(panel(comp, other), away.at[:, lanes_of[comp]], in_sem.at[6 + comp]))
+    for copy in staged:
+        copy.start()
 
     def centre(zi, zj):
         delta = (zj - zi) % NZ
@@ -101,15 +106,6 @@
     for plane in range(NX):
         for zl in range(2):
             pair_dests.append((plane, zl) + pair_dest(plane, zl))
-    offsets = ((0, 0), (0, 1), (-1, 1), (-1, 2), (2, -2), (2, -1), (1, -1), (1, 0))
-    pair_sources = []
-    for delta in range(NZ):
-        zi, zj = (z + offsets[delta][0]) % NZ, (z + offsets[delta][1]) % NZ
-        if 1 <= delta <= 3:
-            pair_sources.append(dev(zi // 2, yh, yl, zj, core))
-        else:
-            pair_sources.append(dev(zi // 2, yl, yh, zj, core))
-
     up = [dev(plane, yh, x // 2, z, core) for plane in range(NX)]
     down = [dev(2 * yl + k // 2, yh, k % 2, z, core) for k in range(4)]
 
@@ -120,29 +116,23 @@
 
     partner = dev(x, yh, other, z, core)
     diagonal = {d: dev(x, yh, other, (z + d) % NZ, core) for d in (1, -1)}
+    y_near = [odev(dy, 0)[2] for dy in (1, 3)]
+    across = dev(x, 1 - yh, other, z, core)
+    sibling = dev(x, yh, yl, z, 1 - core)
+    z_near = [zdev(d) for d in (1, -1, 2, -2)]
+    xy_near = [dev((x + dx) % NX, yh, lo, z, core) for dx in (2, 1, 3) for lo in (other, yl)]
+    near = xy_near + [diagonal[1], diagonal[-1], partner, across, sibling] + z_near
     barrier = pltpu.get_barrier_semaphore()
-    expected = jnp.int32(NZ - 1 + NO - 1 + 2 + 8)
-    for dest in (partner, zdev(1), zdev(-1), diagonal[1], diagonal[-1]):
+    for dest in near:
         pl.semaphore_signal(barrier, inc=1, device_id=dest, device_id_type=MESH)
-    for d in z_steps[:-2]:
-        pl.semaphore_signal(barrier, inc=1, device_id=zdev(d), device_id_type=MESH)
-    for step in o_steps:
-        pl.semaphore_signal(barrier, inc=1, device_id=odev(*step)[2], device_id_type=MESH)
-    expected = expected + 1
-    for dest in up + down:
-        @pl.when(jnp.logical_not(is_me(dest)))
-        def _(dest=dest):
-            pl.semaphore_signal(barrier, inc=1, device_id=dest, device_id_type=MESH)
-        expected = expected - is_me(dest).astype(jnp.int32)
-    for delta, source in enumerate(pair_sources):
-        if not 1 <= delta <= 3:
-            @pl.when(jnp.logical_not(is_me(source)))
-            def _(source=source):
-                pl.semaphore_signal(barrier, inc=1, device_id=source, device_id_type=MESH)
-    for plane, zl, delta, dest in pair_dests:
-        swap = jnp.logical_or(delta == 0, delta >= 4)
-        expected = expected + jnp.logical_and(swap, jnp.logical_not(is_me(dest))).astype(jnp.int32)
-    pl.semaphore_wait(barrier, expected)
+    for copy in staged:
+        copy.wait()
+    pl.semaphore_wait(barrier, len(near))
+
+    def pass_token(k, dests):
+        for dest in dests:
+            pl.semaphore_signal(tokens.at[k], inc=1, device_id=dest, device_id_type=MESH)
+
 
     def send(src, dst, s_sem, r_sem, dest):
         copy = pltpu.make_async_remote_copy(
@@ -150,8 +140,6 @@
         )
         copy.start()
         return copy
-
-    lanes_of = [pl.ds(comp * NP, NP) for comp in range(2)]
 
     def send_or_keep(src, dst, s_sem, r_sem, dest):
         mine = is_me(dest)
@@ -174,13 +162,14 @@
     def launch(k, comp, src, dst, dest):
         send(src, dst.at[:, lanes_of[comp]], gs_sem.at[comp, k], gr_sem.at[comp, k], dest)
 
+    own = u.at[yl, 0, 0]
     for comp in range(2):
-        launch(1, comp, panel(comp, yl), x_left.at[1, yl], zdev(1))
-        launch(2, comp, panel(comp, yl), u.at[yl, 1, 0], zdev(-1))
-        launch(0, comp, panel(comp, other), u.at[yl, 0, 0], partner)
+        launch(1, comp, own.at[:, lanes_of[comp]], x_left.at[1, yl], zdev(1))
+        launch(2, comp, own.at[:, lanes_of[comp]], u.at[yl, 1, 0], zdev(-1))
+        launch(0, comp, away.at[:, lanes_of[comp]], u.at[yl, 0, 0], partner)
     for comp in range(2):
-        launch(3, comp, panel(comp, other), x_left.at[1, yl], diagonal[1])
-        launch(4, comp, panel(comp, other), u.at[yl, 1, 0], diagonal[-1])
+        launch(3, comp, away.at[:, lanes_of[comp]], x_left.at[1, yl], diagonal[1])
+        launch(4, comp, away.at[:, lanes_of[comp]], u.at[yl, 1, 0], diagonal[-1])
 
     def build_turned(lo, j):
         u[lo, j, 1, :, 0:NP] = -u[lo, j, 0, :, NP : 2 * NP]
@@ -190,10 +179,10 @@
         for lo in range(2):
             x_psd[g, lo] = (x_left[g, lo].astype(F32) * psd2).astype(BF16)
 
-    def correlate(g):
+    def correlate(g, halves):
         count = 2 if g < 2 else 1
         left = x_psd[g].reshape(2 * ST, 2 * NP)
-        for lo in range(2):
+        for lo in halves:
             right = u[lo, FIRST_J[g] : FIRST_J[g] + count].reshape(count * 2 * ST, 2 * NP)
             product = lax.dot_general(left, right, (((1,), (1,)), ((), ())), preferred_element_type=F32)
             if count == 1:
@@ -212,6 +201,8 @@
             arrive(at + 1, comp, piece)
             launch(at + 5, comp, piece.at[:, lanes_of[comp]], u.at[half, 2, 0], zdev(-1))
 
+    pass_token(0, z_near)
+
     obs_copy.wait()
     w_copy.wait()
     for zl in range(2):
@@ -219,25 +210,28 @@
         for f in range(NX):
             real = w * obs_v[f, 0, :, zl * ST : (zl + 1) * ST]
             imag = w * obs_v[f, 1, :, zl * ST : (zl + 1) * ST]
-            msg[f, zl] = jnp.concatenate([real, imag, w, w], axis=1)
-
+            msg[f, zl] = jnp.concatenate([real, imag, w, w], axis=1).astype(BF16)
+
+    pl.semaphore_wait(tokens.at[0], len(z_near))
+    pass_token(1, y_near)
     wait_bytes(l_in, lr_sem.at[0])
     for d in z_steps:
         send(l_in, l_z.at[z], ls2_sem.at[0], lr_sem.at[1], zdev(d))
     l_z[z] = l_in[...]
     pass_on(yl, 1)
-    wait_bytes(u.at[yl, 0, 0], in_sem.at[2])
     pass_on(other, 3)
-    wait_bytes(l_z.at[pl.ds(0, NZ - 1)], lr_sem.at[1])
+    pl.semaphore_wait(tokens.at[1], len(y_near))
+    for comp in range(2):
+        arrive(0, comp, u.at[other, 0, 0])
+    pass_token(2, [sibling])
     for k, (plane, zl, delta, dest) in enumerate(pair_dests):
         send_or_keep(msg.at[plane, zl], e_in.at[delta], es_sem.at[k], er_sem.at[0], dest)
-    for comp in range(2):
-        arrive(0, comp, u.at[other, 0, 0])
     for lo in range(2):
         x_left[0, lo] = u[lo, 0, 0]
         build_turned(lo, 0)
         build_turned(lo, 1)
 
+    wait_bytes(l_z.at[pl.ds(0, NZ - 1)], lr_sem.at[1])
     for zz in range(NZ):
         for k in range(4):
             l_rows[k * NZ + zz : k * NZ + zz + 1, :] = l_z[zz, k]
@@ -254,7 +248,9 @@
     build_weighted(0, psd2)
 
     build_weighted(1, psd2)
-    correlate(0)
+    correlate(0, (yl, other))
+
+    pl.semaphore_wait(tokens.at[2], 1)
 
     for half, at in ((yl, 5), (other, 7)):
         for comp in range(2):
@@ -263,22 +259,21 @@
     for lo in range(2):
         build_turned(lo, 2)
     build_weighted(2, psd2)
-    correlate(1)
-    correlate(2)
 
     def pair_terms():
         wait_bytes(e_in, er_sem.at[0])
         lane_at = lax.broadcasted_iota(jnp.int32, (ST, 128), 1)
-        same = (lane_at % ST == lax.broadcasted_iota(jnp.int32, (ST, 128), 0)).astype(F32)
+        same = (lane_at % ST == lax.broadcasted_iota(jnp.int32, (ST, 128), 0)).astype(BF16)
         part_at = lane_at // ST
 
         def turned(block):
-            full = lax.dot_general(block, same, (((0,), (0,)), ((), ())), precision=HIGHEST, preferred_element_type=F32)
+            full = lax.dot_general(block, same, (((0,), (0,)), ((), ())), preferred_element_type=F32)
             result = jnp.where(part_at == 0, full[0:ST], full[ST : 2 * ST])
             result = jnp.where(part_at == 2, full[2 * ST : 3 * ST], result)
             return jnp.where(part_at == 3, full[3 * ST : 4 * ST], result)
 
         def conj(block):
+            block = block.astype(F32)
             return jnp.where(part_at == 1, -block, block)
 
         slots = (
@@ -310,9 +305,13 @@
     def exchange_rest(it, psd):
         phase = lambda k: (ph_s.at[it, k], ph_r.at[it, k])
         s_sem, r_sem = phase(0)
-        for k, step in enumerate(o_steps):
-            to_y, to_core, dest = odev(*step)
-            send(c_part.at[to_y % 2, :, to_y // 2, to_core], rs.at[it, k], s_sem, r_sem, dest)
+        for half, odd in ((yl, 0), (other, 1)):
+            for g in range(1 if it == 0 else 0, 3):
+                correlate(g, (half,))
+            for k, step in enumerate(o_steps):
+                if step[0] % 2 == odd:
+                    to_y, to_core, dest = odev(*step)
+                    send(c_part.at[half, :, to_y // 2, to_core], rs.at[it, k], s_sem, r_sem, dest)
         total = c_part[yl, :, yh, core].astype(F32)
         if it == 0:
             pair_terms()
@@ -359,7 +358,9 @@
         return QUAD * psd * summed
 
     def start_mean(it, gradient):
-        squares = jnp.broadcast_to(jnp.sum(gradient * gradient, axis=1, keepdims=True), (1, 128))
+        squares = gradient[:, 0:128] * gradient[:, 0:128]
+        for k in range(1, NP // 128):
+            squares = squares + gradient[:, k * 128 : (k + 1) * 128] * gradient[:, k * 128 : (k + 1) * 128]
         s_mine[it] = squares
         for step in s_steps:
             send(s_mine.at[it], s_all.at[it, mine_at], ph_s.at[it, 3], ph_r.at[it, 3], sdev(*step))
@@ -367,8 +368,8 @@
 
     def finish_mean(it):
         wait_bytes(s_all.at[it, pl.ds(0, NS - 1)], ph_r.at[it, 3])
-        total = jnp.sum(s_all[it], axis=0)
-        return jnp.sqrt(total / ENTRIES + EPSILON)[:, 0:1]
+        total = jnp.sum(jnp.sum(s_all[it], axis=0), axis=1, keepdims=True)
+        return jnp.sqrt(total / ENTRIES + EPSILON)
 
     gradient = exchange_rest(0, psd)
     start_mean(0, gradient)
@@ -378,7 +379,6 @@
     psd2 = jnp.concatenate([psd, psd], axis=1)
     for g in range(3):
         build_weighted(g, psd2)
-        correlate(g)
     m_mine[...] = log_field
     for k in range(4):
         send_or_keep(m_mine, m_in.at[x], ms_sem.at[k], mr_sem.at[0], down[k])
@@ -430,11 +430,12 @@
             vmem((2, 3, 2, ST, 2 * NP), BF16),
             vmem((3, 2, ST, 2 * NP), BF16),
             vmem((3, 2, ST, 2 * NP), BF16),
+            vmem((ST, 2 * NP), BF16),
             vmem((1, NX, RUN), F32),
             vmem((NX, 2, ST, 2 * ST), F32),
             vmem((ST, 2 * ST), jnp.int32),
-            vmem((NX, 2, ST, 128), F32),
-            vmem((NZ, ST, 128), F32),
+            vmem((NX, 2, ST, 128), BF16),
+            vmem((NZ, ST, 128), BF16),
             vmem((3, ST, 128), F32),
             vmem((3, ST, 128), F32),
             vmem((NX, 1, 128), F32),
@@ -455,7 +456,7 @@
             vmem((NX, 1, NP), F32),
             vmem((8, NP), F32),
             vmem((8, NP), F32),
-            dma((4,)),
+            dma((8,)),
             dma((2, 9)),
             dma((2, 9)),
             dma((1,)),
@@ -463,6 +464,7 @@
             dma((2,)),
             dma((4,)),
             dma((1,)),
+            pltpu.SemaphoreType.REGULAR((3,)),
             dma((ITERS, 4)),
             dma((ITERS, 4)),
             dma((1,)),

time: 61.8 us -> 60.6 us (0.981)
  Pallas kernels: 60.4 us -> 59.2 us
    pallas_call x1, Pallas kernels: 60.4 us -> 59.2 us  [body(): pl.pallas_call(kernel, out_shape=jax.ShapeDtypeStruct(log_psd.shape, F32)...]
where the time goes in v4:
time: 60.6 us; the launch traced here: 60.5 us
  Pallas kernels  59.2 us (98%)
  local copies, waits for them, and re-layouts  1.26 us (2%)
    pallas_call x1, Pallas kernels, body(): pl.pallas_call(kernel, out_shape=jax.ShapeDtypeStruct(log_psd.shape, F32)...  59.2 us
    unnamed x1, local copies, waits for them, and re-layouts  1.26 us

profile of v4, /device:TPU:1, one launch (start us, length us, event | category | flops | bytes accessed | tf_op | source)
XLA Modules:
  0.0 60.5 jit_solution(9192914276456881604)
XLA Ops:
  0.0 59.2 %shard_map.46 = f32[1,4,24]{2,1,0:T(4,128)} custom-call(bf16[4,2,32,3072]{3,2,1,0:T(8,128)(2,1)} %green.1, f32[1,4,24]{2,1,0:T(4,128)} %logp.1, f32[4,2,32,64]{3,2,1,0:T(8,128)} %bitcast.2, s32[32,64]{1,0:T(8,128)} %bitcast.3), custom_call_target="tpu_custom_call" | custom-call | tf_op jit(solution)/shard_map/pallas_call | solution.py:419
  59.2 1.3 %copy.6 = f32[1,4,24]{2,1,0:T(4,128)} copy(f32[1,4,24]{2,1,0:T(4,128)} %shard_map.46) | data formatting | bytes 768

commit v5 on v4

--- a/solution.py
+++ b/solution.py
@@ -25,7 +25,7 @@
 EPSILON = 1e-06
 DESCENT = 0.1
 
-FIRST_J = (0, 1, 2)
+PAIRS = ((0, 0), (0, 1), (1, 1), (1, 2), (2, 2))
 
 
 def wait_bytes(ref, sem):
@@ -35,10 +35,10 @@
 def kernel(
     green, logp, obs, weights, out,
     u, x_left, x_psd, away, log_v, obs_v, w_v, msg, e_in, d_all, w_all,
-    l_src, l_in, l_z, l_rows, c_part, rs, b_out, b_full, g_mine, g_all, s_mine, s_all,
+    l_src, l_in, l_z, l_rows, pair_rows, pair_all, c_part, core_in, y_all, b_full, g_mine, g_all, s_mine, s_all,
     m_mine, o_mine, m_in, o_in, rows_m, rows_o,
     in_sem, gr_sem, gs_sem, er_sem, es_sem, lr_sem, ls_sem, ls2_sem,
-    tokens, ph_r, ph_s, mr_sem, ms_sem, or_sem, os_sem,
+    tokens, pt_sem, ph_r, ph_s, mr_sem, ms_sem, or_sem, os_sem,
 ):
     row = lax.axis_index("row")
     col = lax.axis_index("col")
@@ -85,7 +85,7 @@
     lanes_of = [pl.ds(comp * NP, NP) for comp in range(2)]
     staged = []
     for comp in range(2):
-        staged.append(pltpu.make_async_copy(panel(comp, yl), u.at[yl, 0, 0, :, lanes_of[comp]], in_sem.at[4 + comp]))
+        staged.append(pltpu.make_async_copy(panel(comp, yl), u.at[0, yl, 0, :, lanes_of[comp]], in_sem.at[4 + comp]))
         staged.append(pltpu.make_async_copy(panel(comp, other), away.at[:, lanes_of[comp]], in_sem.at[6 + comp]))
     for copy in staged:
         copy.start()
@@ -162,32 +162,33 @@
     def launch(k, comp, src, dst, dest):
         send(src, dst.at[:, lanes_of[comp]], gs_sem.at[comp, k], gr_sem.at[comp, k], dest)
 
-    own = u.at[yl, 0, 0]
+    own = u.at[0, yl, 0]
     for comp in range(2):
         launch(1, comp, own.at[:, lanes_of[comp]], x_left.at[1, yl], zdev(1))
-        launch(2, comp, own.at[:, lanes_of[comp]], u.at[yl, 1, 0], zdev(-1))
-        launch(0, comp, away.at[:, lanes_of[comp]], u.at[yl, 0, 0], partner)
+        launch(2, comp, own.at[:, lanes_of[comp]], u.at[1, yl, 0], zdev(-1))
+        launch(0, comp, away.at[:, lanes_of[comp]], u.at[0, yl, 0], partner)
     for comp in range(2):
         launch(3, comp, away.at[:, lanes_of[comp]], x_left.at[1, yl], diagonal[1])
-        launch(4, comp, away.at[:, lanes_of[comp]], u.at[yl, 1, 0], diagonal[-1])
+        launch(4, comp, away.at[:, lanes_of[comp]], u.at[1, yl, 0], diagonal[-1])
 
     def build_turned(lo, j):
-        u[lo, j, 1, :, 0:NP] = -u[lo, j, 0, :, NP : 2 * NP]
-        u[lo, j, 1, :, NP : 2 * NP] = u[lo, j, 0, :, 0:NP]
+        u[j, lo, 1, :, 0:NP] = -u[j, lo, 0, :, NP : 2 * NP]
+        u[j, lo, 1, :, NP : 2 * NP] = u[j, lo, 0, :, 0:NP]
 
     def build_weighted(g, psd2):
         for lo in range(2):
             x_psd[g, lo] = (x_left[g, lo].astype(F32) * psd2).astype(BF16)
 
-    def correlate(g, halves):
-        count = 2 if g < 2 else 1
-        left = x_psd[g].reshape(2 * ST, 2 * NP)
-        for lo in halves:
-            right = u[lo, FIRST_J[g] : FIRST_J[g] + count].reshape(count * 2 * ST, 2 * NP)
-            product = lax.dot_general(left, right, (((1,), (1,)), ((), ())), preferred_element_type=F32)
-            if count == 1:
-                product = jnp.concatenate([product, jnp.zeros_like(product)], axis=1)
-            c_part[lo, g] = product.reshape(2, 2, 16, 128).astype(BF16)
+    def correlate(it, j):
+        tiles = [k for k, pair in enumerate(PAIRS) if pair[1] == j]
+        first = PAIRS[tiles[0]][0]
+        left = x_psd[first : first + len(tiles)].reshape(len(tiles) * 2 * ST, 2 * NP)
+        right = u[j].reshape(4 * ST, 2 * NP)
+        product = lax.dot_general(left, right, (((1,), (1,)), ((), ())), preferred_element_type=F32)
+        for k, tile in enumerate(tiles):
+            block = product[k * 2 * ST : (k + 1) * 2 * ST].reshape(2, 2, 16, 128).astype(BF16)
+            for half in range(2):
+                c_part[it, half, tile] = block[:, half]
 
     def arrive(k, comp, dst):
         wait_bytes(dst.at[:, lanes_of[comp]], gr_sem.at[comp, k])
@@ -197,9 +198,9 @@
             piece = x_left.at[1, half]
             arrive(at, comp, piece)
             launch(at + 4, comp, piece.at[:, lanes_of[comp]], x_left.at[2, half], zdev(1))
-            piece = u.at[half, 1, 0]
+            piece = u.at[1, half, 0]
             arrive(at + 1, comp, piece)
-            launch(at + 5, comp, piece.at[:, lanes_of[comp]], u.at[half, 2, 0], zdev(-1))
+            launch(at + 5, comp, piece.at[:, lanes_of[comp]], u.at[2, half, 0], zdev(-1))
 
     pass_token(0, z_near)
 
@@ -222,12 +223,11 @@
     pass_on(other, 3)
     pl.semaphore_wait(tokens.at[1], len(y_near))
     for comp in range(2):
-        arrive(0, comp, u.at[other, 0, 0])
-    pass_token(2, [sibling])
+        arrive(0, comp, u.at[0, other, 0])
     for k, (plane, zl, delta, dest) in enumerate(pair_dests):
         send_or_keep(msg.at[plane, zl], e_in.at[delta], es_sem.at[k], er_sem.at[0], dest)
     for lo in range(2):
-        x_left[0, lo] = u[lo, 0, 0]
+        x_left[0, lo] = u[0, lo, 0]
         build_turned(lo, 0)
         build_turned(lo, 1)
 
@@ -248,17 +248,17 @@
     build_weighted(0, psd2)
 
     build_weighted(1, psd2)
-    correlate(0, (yl, other))
-
-    pl.semaphore_wait(tokens.at[2], 1)
+    correlate(0, 0)
+    correlate(0, 1)
 
     for half, at in ((yl, 5), (other, 7)):
         for comp in range(2):
             arrive(at, comp, x_left.at[2, half])
-            arrive(at + 1, comp, u.at[half, 2, 0])
+            arrive(at + 1, comp, u.at[2, half, 0])
     for lo in range(2):
         build_turned(lo, 2)
     build_weighted(2, psd2)
+    correlate(0, 2)
 
     def pair_terms():
         wait_bytes(e_in, er_sem.at[0])
@@ -276,18 +276,35 @@
             block = block.astype(F32)
             return jnp.where(part_at == 1, -block, block)
 
-        slots = (
-            (conj(e_in[0]), turned(e_in[1]) + conj(e_in[7])),
-            (turned(e_in[2]) + conj(e_in[6]), turned(e_in[3]) + conj(e_in[5])),
-            (conj(e_in[4]), jnp.zeros((ST, 128), F32)),
+        blocks = (
+            conj(e_in[0]),
+            turned(e_in[1]) + conj(e_in[7]),
+            turned(e_in[2]) + conj(e_in[6]),
+            turned(e_in[3]) + conj(e_in[5]),
+            conj(e_in[4]),
         )
-        low = lane_at < 2 * ST
-        for g, (first, second) in enumerate(slots):
-            d_all[g] = jnp.where(low, first, pltpu.roll(second, 64, 1))
-            w_all[g] = jnp.where(low, pltpu.roll(first, 64, 1), second) * QUAD
+        for tile, block in enumerate(blocks):
+            pair_rows[tile] = jnp.where(yl == 0, block, pltpu.roll(block, 64, 1))
+        own_rows = pl.ds(pl.multiple_of(core * 16, 16), 16)
+        pair_all[y_at] = pair_rows[:, own_rows, :].astype(BF16)
+        for dy in (2, 1, 3):
+            send(pair_all.at[y_at], pair_all.at[y_at], pt_sem.at[0], pt_sem.at[1], odev(dy, 0)[2])
+
+    def pair_tiles():
+        wait_bytes(pair_all.at[pl.ds(0, 3)], pt_sem.at[1])
+        low = lax.broadcasted_iota(jnp.int32, (16, 128), 1) < 64
+        for tile in range(len(PAIRS)):
+            for hi in range(2):
+                first = pair_all[2 * hi, tile].astype(F32)
+                second = pair_all[2 * hi + 1, tile].astype(F32)
+                d_all[tile, hi] = jnp.where(low, first, second)
+                w_all[tile, hi] = jnp.where(low, pltpu.roll(first, 64, 1), pltpu.roll(second, 64, 1)) * QUAD
 
     def finish_phase(it, phase):
-        sizes = (rs.at[it], rs.at[it], g_all.at[it, pl.ds(0, NZ - 1)], s_all.at[it, pl.ds(0, NS - 1)])
+        sizes = (
+            core_in.at[it], y_all.at[it, pl.ds(0, 3)], g_all.at[it, pl.ds(0, NZ - 1)],
+            s_all.at[it, pl.ds(0, NS - 1)], core_in.at[it],
+        )
         wait_bytes(sizes[phase], ph_s.at[it, phase])
 
     def finish_start():
@@ -299,35 +316,32 @@
         wait_bytes(l_z.at[pl.ds(0, NZ - 1)], ls2_sem.at[0])
         for k, (plane, zl, delta, dest) in enumerate(pair_dests):
             finish_send(msg.at[plane, zl], es_sem.at[k], dest)
-        for phase in range(1, 4):
+        wait_bytes(pair_all.at[pl.ds(0, 3)], pt_sem.at[0])
+        for phase in range(5):
             finish_phase(0, phase)
 
     def exchange_rest(it, psd):
         phase = lambda k: (ph_s.at[it, k], ph_r.at[it, k])
         s_sem, r_sem = phase(0)
-        for half, odd in ((yl, 0), (other, 1)):
-            for g in range(1 if it == 0 else 0, 3):
-                correlate(g, (half,))
-            for k, step in enumerate(o_steps):
-                if step[0] % 2 == odd:
-                    to_y, to_core, dest = odev(*step)
-                    send(c_part.at[half, :, to_y // 2, to_core], rs.at[it, k], s_sem, r_sem, dest)
-        total = c_part[yl, :, yh, core].astype(F32)
+        send(c_part.at[it, 1 - core], core_in.at[it], s_sem, r_sem, sibling)
+        wait_bytes(core_in.at[it], r_sem)
+        y_all[it, y_at] = (c_part[it, core].astype(F32) + core_in[it].astype(F32)).astype(BF16)
+        s_sem, r_sem = phase(1)
+        for dy in (2, 1, 3):
+            send(y_all.at[it, y_at], y_all.at[it, y_at], s_sem, r_sem, odev(dy, 0)[2])
         if it == 0:
             pair_terms()
+            pair_tiles()
         else:
             finish_start()
-        wait_bytes(rs.at[it], r_sem)
-        for d in range(NO - 1):
-            total = total + rs[it, d].astype(F32)
-        own_rows = pl.ds(pl.multiple_of(core * 16, 16), 16)
-        b_out[it] = (w_all[:, own_rows, :] * total - d_all[:, own_rows, :]).astype(BF16)
-        s_sem, r_sem = phase(1)
-        for step in o_steps:
-            send(b_out.at[it], b_full.at[it, yl, :, yh, core], s_sem, r_sem, odev(*step)[2])
-        b_full[it, yl, :, yh, core] = b_out[it]
-        finish_phase(it, 0)
-        wait_bytes(rs.at[it], r_sem)
+        wait_bytes(y_all.at[it, pl.ds(0, 3)], r_sem)
+        total = y_all[it, 0].astype(F32)
+        for k in range(1, 4):
+            total = total + y_all[it, k].astype(F32)
+        b_full[it, core] = (w_all[...] * total - d_all[...]).astype(BF16)
+        s_sem, r_sem = phase(4)
+        send(b_full.at[it, core], b_full.at[it, core], s_sem, r_sem, sibling)
+        wait_bytes(core_in.at[it], r_sem)
 
         width = 384
         terms = []
@@ -335,12 +349,17 @@
             lanes = slice(c * width, (c + 1) * width)
             term = jnp.zeros((1, width), F32)
             for g in range(3):
-                count = 2 if g < 2 else 1
-                field = jnp.zeros((2 * ST, width), F32)
-                for lo in range(2):
-                    b = b_full[it, lo, g].reshape(2 * ST, 128)[:, 0 : count * 2 * ST]
-                    right = u[lo, FIRST_J[g] : FIRST_J[g] + count, :, :, lanes].reshape(count * 2 * ST, width)
-                    field = field + jnp.dot(b, right, preferred_element_type=F32)
+                tiles = [k for k, pair in enumerate(PAIRS) if pair[0] == g]
+                first = PAIRS[tiles[0]][1]
+                b = jnp.concatenate(
+                    [
+                        jnp.concatenate([b_full[it, half, tile, hi] for hi in range(2) for half in range(2)], axis=0)
+                        for tile in tiles
+                    ],
+                    axis=1,
+                )
+                right = u[first : first + len(tiles), :, :, :, lanes].reshape(len(tiles) * 4 * ST, width)
+                field = jnp.dot(b, right, preferred_element_type=F32)
                 left = x_left[g, :, :, lanes].reshape(2 * ST, width).astype(F32)
                 term = term + jnp.sum(left * field, axis=0, keepdims=True)
             terms.append(term)
@@ -379,6 +398,8 @@
     psd2 = jnp.concatenate([psd, psd], axis=1)
     for g in range(3):
         build_weighted(g, psd2)
+    for j in range(3):
+        correlate(1, j)
     m_mine[...] = log_field
     for k in range(4):
         send_or_keep(m_mine, m_in.at[x], ms_sem.at[k], mr_sem.at[0], down[k])
@@ -405,9 +426,8 @@
     own_gradient = run_of_points(rows_o, o_in)
     out[0] = own_field - DESCENT * own_gradient / finish_mean(1)
 
-    finish_phase(1, 1)
-    finish_phase(1, 2)
-    finish_phase(1, 3)
+    for phase in range(5):
+        finish_phase(1, phase)
     for k in range(4):
         finish_send(m_mine, ms_sem.at[k], down[k])
         finish_send(o_mine, os_sem.at[k], down[k])
@@ -427,7 +447,7 @@
         ],
         out_specs=pl.BlockSpec(memory_space=pltpu.VMEM),
         scratch_shapes=[
-            vmem((2, 3, 2, ST, 2 * NP), BF16),
+            vmem((3, 2, 2, ST, 2 * NP), BF16),
             vmem((3, 2, ST, 2 * NP), BF16),
             vmem((3, 2, ST, 2 * NP), BF16),
             vmem((ST, 2 * NP), BF16),
@@ -436,16 +456,18 @@
             vmem((ST, 2 * ST), jnp.int32),
             vmem((NX, 2, ST, 128), BF16),
             vmem((NZ, ST, 128), BF16),
-            vmem((3, ST, 128), F32),
-            vmem((3, ST, 128), F32),
+            vmem((5, 2, 16, 128), F32),
+            vmem((5, 2, 16, 128), F32),
             vmem((NX, 1, 128), F32),
             vmem((4, 1, 128), F32),
             vmem((NZ, 4, 1, 128), F32),
             vmem((32, 128), F32),
-            vmem((2, 3, 2, 2, 16, 128), BF16),
-            vmem((ITERS, NO - 1, 3, 16, 128), BF16),
-            vmem((ITERS, 3, 16, 128), BF16),
-            vmem((ITERS, 2, 3, 2, 2, 16, 128), BF16),
+            vmem((5, ST, 128), F32),
+            vmem((4, 5, 16, 128), BF16),
+            vmem((ITERS, 2, 5, 2, 16, 128), BF16),
+            vmem((ITERS, 5, 2, 16, 128), BF16),
+            vmem((ITERS, 4, 5, 2, 16, 128), BF16),
+            vmem((ITERS, 2, 5, 2, 16, 128), BF16),
             vmem((ITERS, 1, NP), F32),
             vmem((ITERS, NZ, 1, NP), F32),
             vmem((ITERS, 1, 128), F32),
@@ -464,9 +486,10 @@
             dma((2,)),
             dma((4,)),
             dma((1,)),
-            pltpu.SemaphoreType.REGULAR((3,)),
-            dma((ITERS, 4)),
-            dma((ITERS, 4)),
+            pltpu.SemaphoreType.REGULAR((2,)),
+            dma((2,)),
+            dma((ITERS, 5)),
+            dma((ITERS, 5)),
             dma((1,)),
             dma((4,)),
             dma((1,)),

time: 60.6 us -> 58.3 us (0.962)
  Pallas kernels: 59.2 us -> 56.9 us
    pallas_call x1, Pallas kernels: 59.2 us -> 56.9 us  [body(): pl.pallas_call(kernel, out_shape=jax.ShapeDtypeStruct(log_psd.shape, F32)...]
where the time goes in v5:
time: 58.3 us; the launch traced here: 58.1 us
  Pallas kernels  56.9 us (98%)
  local copies, waits for them, and re-layouts  1.26 us (2%)
    pallas_call x1, Pallas kernels, body(): pl.pallas_call(kernel, out_shape=jax.ShapeDtypeStruct(log_psd.shape, F32)...  56.9 us
    unnamed x1, local copies, waits for them, and re-layouts  1.26 us

profile of v5, /device:TPU:1, one launch (start us, length us, event | category | flops | bytes accessed | tf_op | source)
XLA Modules:
  0.0 58.1 jit_solution(15662284844043188604)
XLA Ops:
  0.0 56.9 %shard_map.46 = f32[1,4,24]{2,1,0:T(4,128)} custom-call(bf16[4,2,32,3072]{3,2,1,0:T(8,128)(2,1)} %green.1, f32[1,4,24]{2,1,0:T(4,128)} %logp.1, f32[4,2,32,64]{3,2,1,0:T(8,128)} %bitcast.2, s32[32,64]{1,0:T(8,128)} %bitcast.3), custom_call_target="tpu_custom_call" | custom-call | tf_op jit(solution)/shard_map/pallas_call | solution.py:439
  56.9 1.3 %copy.6 = f32[1,4,24]{2,1,0:T(4,128)} copy(f32[1,4,24]{2,1,0:T(4,128)} %shard_map.46) | data formatting | bytes 768

commit v6 on v5

--- a/solution.py
+++ b/solution.py
@@ -189,6 +189,20 @@
             block = product[k * 2 * ST : (k + 1) * 2 * ST].reshape(2, 2, 16, 128).astype(BF16)
             for half in range(2):
                 c_part[it, half, tile] = block[:, half]
+
+    def sum_sems(it, first, stage):
+        k = stage if first == 0 else 5 + stage
+        return ph_s.at[it, k], ph_r.at[it, k]
+
+    def sum_tiles(it, first, last):
+        tiles = pl.ds(first, last - first)
+        s_sem, r_sem = sum_sems(it, first, 0)
+        send(c_part.at[it, 1 - core, tiles], core_in.at[it, tiles], s_sem, r_sem, sibling)
+        wait_bytes(core_in.at[it, tiles], r_sem)
+        y_all[it, y_at, tiles] = (c_part[it, core, tiles].astype(F32) + core_in[it, tiles].astype(F32)).astype(BF16)
+        s_sem, r_sem = sum_sems(it, first, 1)
+        for dy in (2, 1, 3):
+            send(y_all.at[it, y_at, tiles], y_all.at[it, y_at, tiles], s_sem, r_sem, odev(dy, 0)[2])
 
     def arrive(k, comp, dst):
         wait_bytes(dst.at[:, lanes_of[comp]], gr_sem.at[comp, k])
@@ -250,6 +264,7 @@
     build_weighted(1, psd2)
     correlate(0, 0)
     correlate(0, 1)
+    sum_tiles(0, 0, 3)
 
     for half, at in ((yl, 5), (other, 7)):
         for comp in range(2):
@@ -301,11 +316,17 @@
                 w_all[tile, hi] = jnp.where(low, pltpu.roll(first, 64, 1), pltpu.roll(second, 64, 1)) * QUAD
 
     def finish_phase(it, phase):
-        sizes = (
-            core_in.at[it], y_all.at[it, pl.ds(0, 3)], g_all.at[it, pl.ds(0, NZ - 1)],
-            s_all.at[it, pl.ds(0, NS - 1)], core_in.at[it],
-        )
-        wait_bytes(sizes[phase], ph_s.at[it, phase])
+        if phase == 2:
+            wait_bytes(g_all.at[it, pl.ds(0, NZ - 1)], ph_s.at[it, 2])
+        elif phase == 3:
+            wait_bytes(s_all.at[it, pl.ds(0, NS - 1)], ph_s.at[it, 3])
+        elif phase == 4:
+            wait_bytes(core_in.at[it], ph_s.at[it, 4])
+        else:
+            for part in ((0, 3), (3, 5)) if it == 0 else ((0, 5),):
+                tiles = pl.ds(part[0], part[1] - part[0])
+                left = core_in.at[it, tiles] if phase == 0 else y_all.at[it, pl.ds(0, 3), tiles]
+                wait_bytes(left, sum_sems(it, part[0], phase)[0])
 
     def finish_start():
         for comp in range(2):
@@ -322,19 +343,15 @@
 
     def exchange_rest(it, psd):
         phase = lambda k: (ph_s.at[it, k], ph_r.at[it, k])
-        s_sem, r_sem = phase(0)
-        send(c_part.at[it, 1 - core], core_in.at[it], s_sem, r_sem, sibling)
-        wait_bytes(core_in.at[it], r_sem)
-        y_all[it, y_at] = (c_part[it, core].astype(F32) + core_in[it].astype(F32)).astype(BF16)
-        s_sem, r_sem = phase(1)
-        for dy in (2, 1, 3):
-            send(y_all.at[it, y_at], y_all.at[it, y_at], s_sem, r_sem, odev(dy, 0)[2])
+        sum_tiles(it, 3 if it == 0 else 0, 5)
         if it == 0:
             pair_terms()
             pair_tiles()
         else:
             finish_start()
-        wait_bytes(y_all.at[it, pl.ds(0, 3)], r_sem)
+        for part in ((0, 3), (3, 5)) if it == 0 else ((0, 5),):
+            tiles = pl.ds(part[0], part[1] - part[0])
+            wait_bytes(y_all.at[it, pl.ds(0, 3), tiles], sum_sems(it, part[0], 1)[1])
         total = y_all[it, 0].astype(F32)
         for k in range(1, 4):
             total = total + y_all[it, k].astype(F32)
@@ -488,8 +505,8 @@
             dma((1,)),
             pltpu.SemaphoreType.REGULAR((2,)),
             dma((2,)),
-            dma((ITERS, 5)),
-            dma((ITERS, 5)),
+            dma((ITERS, 7)),
+            dma((ITERS, 7)),
             dma((1,)),
             dma((4,)),
             dma((1,)),

time: 58.3 us -> 57.9 us (level)
  no operation moved by 1% of the time
where the time goes in v6:
time: 57.9 us; the launch traced here: 57.8 us
  Pallas kernels  56.5 us (98%)
  local copies, waits for them, and re-layouts  1.26 us (2%)
    pallas_call x1, Pallas kernels, body(): pl.pallas_call(kernel, out_shape=jax.ShapeDtypeStruct(log_psd.shape, F32)...  56.5 us
    unnamed x1, local copies, waits for them, and re-layouts  1.26 us

profile of v6, /device:TPU:1, one launch (start us, length us, event | category | flops | bytes accessed | tf_op | source)
XLA Modules:
  0.0 57.8 jit_solution(11121664134336868901)
XLA Ops:
  0.0 56.5 %shard_map.46 = f32[1,4,24]{2,1,0:T(4,128)} custom-call(bf16[4,2,32,3072]{3,2,1,0:T(8,128)(2,1)} %green.1, f32[1,4,24]{2,1,0:T(4,128)} %logp.1, f32[4,2,32,64]{3,2,1,0:T(8,128)} %bitcast.2, s32[32,64]{1,0:T(8,128)} %bitcast.3), custom_call_target="tpu_custom_call" | custom-call | tf_op jit(solution)/shard_map/pallas_call | solution.py:456
  56.5 1.3 %copy.6 = f32[1,4,24]{2,1,0:T(4,128)} copy(f32[1,4,24]{2,1,0:T(4,128)} %shard_map.46) | data formatting | bytes 768

commit v7 on v6

--- a/solution.py
+++ b/solution.py
@@ -97,9 +97,14 @@
         zc = jnp.where(delta <= 3, zi + from_i, zj + from_j) % NZ
         return delta, zc
 
+    core_rows = pl.ds(pl.multiple_of(core * 16, 16), 16)
+
+    def as_it_is(delta):
+        return jnp.logical_or(delta == 0, delta >= 4)
+
     def pair_dest(plane, zl):
         delta, zc = centre(2 * x + zl, z)
-        swap = jnp.logical_or(delta == 0, delta >= 4)
+        swap = as_it_is(delta)
         return delta, dev(plane, jnp.where(swap, yl, yh), jnp.where(swap, yh, yl), zc, core)
 
     pair_dests = []
@@ -111,6 +116,7 @@
 
     log_copy.wait()
     l_src[...] = jnp.zeros_like(l_src)
+    e_in[...] = jnp.zeros_like(e_in)
     for f in range(NX):
         l_src[f, :, 0:RUN] = log_v[0, f : f + 1, :]
 
@@ -239,7 +245,16 @@
     for comp in range(2):
         arrive(0, comp, u.at[0, other, 0])
     for k, (plane, zl, delta, dest) in enumerate(pair_dests):
-        send_or_keep(msg.at[plane, zl], e_in.at[delta], es_sem.at[k], er_sem.at[0], dest)
+        block = msg.at[plane, zl]
+
+        @pl.when(as_it_is(delta))
+        def _(block=block, delta=delta, k=k, dest=dest):
+            send_or_keep(block.at[core_rows], e_in.at[delta, core_rows], es_sem.at[k], er_sem.at[0], dest)
+
+        @pl.when(jnp.logical_not(as_it_is(delta)))
+        def _(block=block, delta=delta, k=k, dest=dest):
+            send(block, e_in.at[delta], es_sem.at[k], er_sem.at[1], dest)
+
     for lo in range(2):
         x_left[0, lo] = u[0, lo, 0]
         build_turned(lo, 0)
@@ -276,7 +291,8 @@
     correlate(0, 2)
 
     def pair_terms():
-        wait_bytes(e_in, er_sem.at[0])
+        wait_bytes(e_in.at[pl.ds(0, 5), pl.ds(0, 16)], er_sem.at[0])
+        wait_bytes(e_in.at[pl.ds(0, 3)], er_sem.at[1])
         lane_at = lax.broadcasted_iota(jnp.int32, (ST, 128), 1)
         same = (lane_at % ST == lax.broadcasted_iota(jnp.int32, (ST, 128), 0)).astype(BF16)
         part_at = lane_at // ST
@@ -300,8 +316,7 @@
         )
         for tile, block in enumerate(blocks):
             pair_rows[tile] = jnp.where(yl == 0, block, pltpu.roll(block, 64, 1))
-        own_rows = pl.ds(pl.multiple_of(core * 16, 16), 16)
-        pair_all[y_at] = pair_rows[:, own_rows, :].astype(BF16)
+        pair_all[y_at] = pair_rows[:, core_rows, :].astype(BF16)
         for dy in (2, 1, 3):
             send(pair_all.at[y_at], pair_all.at[y_at], pt_sem.at[0], pt_sem.at[1], odev(dy, 0)[2])
 
@@ -336,7 +351,14 @@
             finish_send(l_src.at[f], ls_sem.at[f], up[f])
         wait_bytes(l_z.at[pl.ds(0, NZ - 1)], ls2_sem.at[0])
         for k, (plane, zl, delta, dest) in enumerate(pair_dests):
-            finish_send(msg.at[plane, zl], es_sem.at[k], dest)
+            @pl.when(as_it_is(delta))
+            def _(block=msg.at[plane, zl, core_rows], k=k, dest=dest):
+                finish_send(block, es_sem.at[k], dest)
+
+            @pl.when(jnp.logical_not(as_it_is(delta)))
+            def _(block=msg.at[plane, zl], k=k):
+                wait_bytes(block, es_sem.at[k])
+
         wait_bytes(pair_all.at[pl.ds(0, 3)], pt_sem.at[0])
         for phase in range(5):
             finish_phase(0, phase)
@@ -498,7 +520,7 @@
             dma((8,)),
             dma((2, 9)),
             dma((2, 9)),
-            dma((1,)),
+            dma((2,)),
             dma((8,)),
             dma((2,)),
             dma((4,)),

time: 57.9 us -> 57 us (0.984)
  Pallas kernels: 56.5 us -> 55.6 us
    pallas_call x1, Pallas kernels: 56.5 us -> 55.6 us  [body(): pl.pallas_call(kernel, out_shape=jax.ShapeDtypeStruct(log_psd.shape, F32)...]
where the time goes in v7:
time: 57 us; the launch traced here: 56.9 us
  Pallas kernels  55.6 us (98%)
  local copies, waits for them, and re-layouts  1.26 us (2%)
    pallas_call x1, Pallas kernels, body(): pl.pallas_call(kernel, out_shape=jax.ShapeDtypeStruct(log_psd.shape, F32)...  55.6 us
    unnamed x1, local copies, waits for them, and re-layouts  1.26 us

profile of v7, /device:TPU:1, one launch (start us, length us, event | category | flops | bytes accessed | tf_op | source)
XLA Modules:
  0.0 56.9 jit_solution(7216205194739330156)
XLA Ops:
  0.0 55.6 %shard_map.46 = f32[1,4,24]{2,1,0:T(4,128)} custom-call(bf16[4,2,32,3072]{3,2,1,0:T(8,128)(2,1)} %green.1, f32[1,4,24]{2,1,0:T(4,128)} %logp.1, f32[4,2,32,64]{3,2,1,0:T(8,128)} %bitcast.2, s32[32,64]{1,0:T(8,128)} %bitcast.3), custom_call_target="tpu_custom_call" | custom-call | tf_op jit(solution)/shard_map/pallas_call | solution.py:478
  55.6 1.3 %copy.6 = f32[1,4,24]{2,1,0:T(4,128)} copy(f32[1,4,24]{2,1,0:T(4,128)} %shard_map.46) | data formatting | bytes 768

commit v8 on v6

--- a/solution.py
+++ b/solution.py
@@ -35,7 +35,7 @@
 def kernel(
     green, logp, obs, weights, out,
     u, x_left, x_psd, away, log_v, obs_v, w_v, msg, e_in, d_all, w_all,
-    l_src, l_in, l_z, l_rows, pair_rows, pair_all, c_part, core_in, y_all, b_full, g_mine, g_all, s_mine, s_all,
+    l_src, l_in, l_z, l_rows, pair_all, c_part, core_in, y_all, b_full, g_mine, g_all, s_mine, s_all,
     m_mine, o_mine, m_in, o_in, rows_m, rows_o,
     in_sem, gr_sem, gs_sem, er_sem, es_sem, lr_sem, ls_sem, ls2_sem,
     tokens, pt_sem, ph_r, ph_s, mr_sem, ms_sem, or_sem, os_sem,
@@ -97,9 +97,14 @@
         zc = jnp.where(delta <= 3, zi + from_i, zj + from_j) % NZ
         return delta, zc
 
+    core_rows = pl.ds(pl.multiple_of(core * 16, 16), 16)
+
+    def as_it_is(delta):
+        return jnp.logical_or(delta == 0, delta >= 4)
+
     def pair_dest(plane, zl):
         delta, zc = centre(2 * x + zl, z)
-        swap = jnp.logical_or(delta == 0, delta >= 4)
+        swap = as_it_is(delta)
         return delta, dev(plane, jnp.where(swap, yl, yh), jnp.where(swap, yh, yl), zc, core)
 
     pair_dests = []
@@ -218,6 +223,16 @@
 
     pass_token(0, z_near)
 
+    lane_at = lax.broadcasted_iota(jnp.int32, (ST, 128), 1)
+    same = (lane_at % ST == lax.broadcasted_iota(jnp.int32, (ST, 128), 0)).astype(BF16)
+    part_at = lane_at // ST
+
+    def turned(block):
+        full = lax.dot_general(block, same, (((0,), (0,)), ((), ())), preferred_element_type=F32)
+        result = jnp.where(part_at == 0, full[0:ST], full[ST : 2 * ST])
+        result = jnp.where(part_at == 2, full[2 * ST : 3 * ST], result)
+        return jnp.where(part_at == 3, full[3 * ST : 4 * ST], result)
+
     obs_copy.wait()
     w_copy.wait()
     for zl in range(2):
@@ -225,7 +240,8 @@
         for f in range(NX):
             real = w * obs_v[f, 0, :, zl * ST : (zl + 1) * ST]
             imag = w * obs_v[f, 1, :, zl * ST : (zl + 1) * ST]
-            msg[f, zl] = jnp.concatenate([real, imag, w, w], axis=1).astype(BF16)
+            block = jnp.concatenate([real, imag, w, w], axis=1).astype(BF16)
+            msg[f, zl] = jnp.where(as_it_is(pair_dests[zl][2]), block.astype(F32), turned(block)).astype(BF16)
 
     pl.semaphore_wait(tokens.at[0], len(z_near))
     pass_token(1, y_near)
@@ -239,7 +255,7 @@
     for comp in range(2):
         arrive(0, comp, u.at[0, other, 0])
     for k, (plane, zl, delta, dest) in enumerate(pair_dests):
-        send_or_keep(msg.at[plane, zl], e_in.at[delta], es_sem.at[k], er_sem.at[0], dest)
+        send_or_keep(msg.at[plane, zl, core_rows], e_in.at[delta], es_sem.at[k], er_sem.at[0], dest)
     for lo in range(2):
         x_left[0, lo] = u[0, lo, 0]
         build_turned(lo, 0)
@@ -277,15 +293,7 @@
 
     def pair_terms():
         wait_bytes(e_in, er_sem.at[0])
-        lane_at = lax.broadcasted_iota(jnp.int32, (ST, 128), 1)
-        same = (lane_at % ST == lax.broadcasted_iota(jnp.int32, (ST, 128), 0)).astype(BF16)
-        part_at = lane_at // ST
-
-        def turned(block):
-            full = lax.dot_general(block, same, (((0,), (0,)), ((), ())), preferred_element_type=F32)
-            result = jnp.where(part_at == 0, full[0:ST], full[ST : 2 * ST])
-            result = jnp.where(part_at == 2, full[2 * ST : 3 * ST], result)
-            return jnp.where(part_at == 3, full[3 * ST : 4 * ST], result)
+        part_at = lax.broadcasted_iota(jnp.int32, (16, 128), 1) // ST
 
         def conj(block):
             block = block.astype(F32)
@@ -293,15 +301,13 @@
 
         blocks = (
             conj(e_in[0]),
-            turned(e_in[1]) + conj(e_in[7]),
-            turned(e_in[2]) + conj(e_in[6]),
-            turned(e_in[3]) + conj(e_in[5]),
+            e_in[1].astype(F32) + conj(e_in[7]),
+            e_in[2].astype(F32) + conj(e_in[6]),
+            e_in[3].astype(F32) + conj(e_in[5]),
             conj(e_in[4]),
         )
         for tile, block in enumerate(blocks):
-            pair_rows[tile] = jnp.where(yl == 0, block, pltpu.roll(block, 64, 1))
-        own_rows = pl.ds(pl.multiple_of(core * 16, 16), 16)
-        pair_all[y_at] = pair_rows[:, own_rows, :].astype(BF16)
+            pair_all[y_at, tile] = jnp.where(yl == 0, block, pltpu.roll(block, 64, 1)).astype(BF16)
         for dy in (2, 1, 3):
             send(pair_all.at[y_at], pair_all.at[y_at], pt_sem.at[0], pt_sem.at[1], odev(dy, 0)[2])
 
@@ -336,7 +342,7 @@
             finish_send(l_src.at[f], ls_sem.at[f], up[f])
         wait_bytes(l_z.at[pl.ds(0, NZ - 1)], ls2_sem.at[0])
         for k, (plane, zl, delta, dest) in enumerate(pair_dests):
-            finish_send(msg.at[plane, zl], es_sem.at[k], dest)
+            finish_send(msg.at[plane, zl, core_rows], es_sem.at[k], dest)
         wait_bytes(pair_all.at[pl.ds(0, 3)], pt_sem.at[0])
         for phase in range(5):
             finish_phase(0, phase)
@@ -472,14 +478,13 @@
             vmem((NX, 2, ST, 2 * ST), F32),
             vmem((ST, 2 * ST), jnp.int32),
             vmem((NX, 2, ST, 128), BF16),
-            vmem((NZ, ST, 128), BF16),
+            vmem((NZ, 16, 128), BF16),
             vmem((5, 2, 16, 128), F32),
             vmem((5, 2, 16, 128), F32),
             vmem((NX, 1, 128), F32),
             vmem((4, 1, 128), F32),
             vmem((NZ, 4, 1, 128), F32),
             vmem((32, 128), F32),
-            vmem((5, ST, 128), F32),
             vmem((4, 5, 16, 128), BF16),
             vmem((ITERS, 2, 5, 2, 16, 128), BF16),
             vmem((ITERS, 5, 2, 16, 128), BF16),

time: 57.9 us -> 56.9 us (0.983)
  Pallas kernels: 56.5 us -> 55.5 us
    pallas_call x1, Pallas kernels: 56.5 us -> 55.5 us  [body(): pl.pallas_call(kernel, out_shape=jax.ShapeDtypeStruct(log_psd.shape, F32)...]
where the time goes in v8:
time: 56.9 us; the launch traced here: 56.8 us
  Pallas kernels  55.5 us (98%)
  local copies, waits for them, and re-layouts  1.26 us (2%)
    pallas_call x1, Pallas kernels, body(): pl.pallas_call(kernel, out_shape=jax.ShapeDtypeStruct(log_psd.shape, F32)...  55.5 us
    unnamed x1, local copies, waits for them, and re-layouts  1.26 us

profile of v8, /device:TPU:1, one launch (start us, length us, event | category | flops | bytes accessed | tf_op | source)
XLA Modules:
  0.0 56.8 jit_solution(14152641277145322097)
XLA Ops:
  0.0 55.5 %shard_map.46 = f32[1,4,24]{2,1,0:T(4,128)} custom-call(bf16[4,2,32,3072]{3,2,1,0:T(8,128)(2,1)} %green.1, f32[1,4,24]{2,1,0:T(4,128)} %logp.1, f32[4,2,32,64]{3,2,1,0:T(8,128)} %bitcast.2, s32[32,64]{1,0:T(8,128)} %bitcast.3), custom_call_target="tpu_custom_call" | custom-call | tf_op jit(solution)/shard_map/pallas_call | solution.py:462
  55.5 1.3 %copy.6 = f32[1,4,24]{2,1,0:T(4,128)} copy(f32[1,4,24]{2,1,0:T(4,128)} %shard_map.46) | data formatting | bytes 768
